TPU v7x, 256 devices: a whole 4x4x8 slice. The times are simulated.
256 devices in a mesh: ctx: 32 (over z, y_hi, core), kvh: 8 (over x, y_lo).
Axes of the slice: x: 4, y: 4 (y_hi: 2, y_lo: 2; y = y_hi * 2 + y_lo), z: 8, core: 2. Of those that a mesh axis runs over, the one named last changes fastest.
Arguments:
- queries: bfloat16 [512, 8192], P('ctx', 'kvh'), may hold values from -200 to 200
- cache_keys: bfloat16 [65536, 1024], P('ctx', 'kvh'), may hold values from -7 to 7
- prefix_values: bfloat16 [65536, 1024], P('ctx', 'kvh'), may hold values from -6 to 6
- candidate_row_keys: bfloat16 [512, 1024], P('ctx', 'kvh'), may hold values from -12 to 12
- candidate_values: bfloat16 [512, 1024], P('ctx', 'kvh'), may hold values from -6 to 6
- prefix_len: int32 [512], P('ctx'), may hold values from 16384 to 65536, as said below
- branch: int32 [512], P('ctx'), may hold values from 0 to 127
- depth: int32 [512], P('ctx'), may hold values from 0 to 15
- out_weight: bfloat16 [8192, 8192], P('kvh', 'ctx'), may hold values from -0.625 to 0.625
Outputs:
- projected: bfloat16 [512, 8192], P('kvh', 'ctx')
Inputs may be any that keep to these rules, and one draw needn't show every extreme that they name: `prefix_len`: the 16 rows of each index of ctx share a longest length, which differs from index to index; some row has length 65536.
All inputs are finite; a program needn't handle non-finite values.
Results may differ from a plain program's by a relative error of at most 0.015.
Values may be sent and summed in bfloat16 or wider, within the bound.
A program may use at most 64 MiB of HBM per device.

v0:
```python
import math

import jax
import jax.numpy as jnp
from jax import lax
from jax.sharding import PartitionSpec as P

HEAD_SIZE = 128
QUERY_PER_KV = 8


NEG = -1e30


def passed_along(block, axis, distance):
    devices = range(lax.axis_size(axis))
    route = [((i - distance) % len(devices), i) for i in devices]
    return lax.ppermute(block, axis, route)


def fold_block(carry, scores, mask, values):
    top, total, acc = carry
    scores = jnp.where(mask, scores, NEG)
    new_top = jnp.maximum(top, jnp.max(scores, axis=-1))
    probs = jnp.where(mask, jnp.exp(scores - new_top[..., None]), 0.0)
    total = jnp.sum(probs, axis=-1)
    acc = jnp.einsum(
        "rkgn,nkd->rkgd", probs.astype(jnp.bfloat16), values, preferred_element_type=jnp.float32
    )
    return (new_top, total, acc)


def move_query(block, way):
    if way == 1:
        return passed_along(block, "ctx", 1)
    return passed_along(block, "ctx", -1)


def local(
    queries,
    cache_keys,
    prefix_values,
    candidate_row_keys,
    candidate_values,
    prefix_len,
    branch,
    depth,
    out_weight,
):
    rows = queries.shape[0]
    shard = cache_keys.shape[0]
    kv_dev = cache_keys.shape[1] // HEAD_SIZE
    cycle = lax.axis_size("ctx")
    here = lax.axis_index("ctx")
    scale = 1.0 / math.sqrt(HEAD_SIZE)
    q_heads = queries.reshape(rows, kv_dev, QUERY_PER_KV, HEAD_SIZE)
    keys_local = cache_keys.reshape(shard, kv_dev, HEAD_SIZE)
    vals_local = prefix_values.reshape(shard, kv_dev, HEAD_SIZE)
    all_len, all_branch, all_depth = (
        lax.all_gather(prefix_len, "ctx", axis=0, tiled=True),
        lax.all_gather(branch, "ctx", axis=0, tiled=True),
        lax.all_gather(depth, "ctx", axis=0, tiled=True),
    )

    def blank(width_g):
        return (
            jnp.full((rows, kv_dev, width_g), NEG, jnp.float32),
            jnp.zeros((rows, kv_dev, width_g), jnp.float32),
            jnp.zeros((rows, kv_dev, width_g, HEAD_SIZE), jnp.float32),
        )

    key_piece = lax.all_gather(candidate_row_keys, "ctx", axis=0, tiled=True)
    value_piece = lax.all_gather(candidate_values, "ctx", axis=0, tiled=True)
    count = key_piece.shape[0]
    scores = (
        jnp.einsum(
            "rkgd,nkd->rkgn",
            q_heads,
            key_piece.reshape(count, kv_dev, HEAD_SIZE),
            preferred_element_type=jnp.float32,
        )
        * scale
    )
    mask = ((all_branch[None, :] == branch[:, None]) & (all_depth[None, :] <= depth[:, None]))[
        :, None, None, :
    ]
    own = fold_block(
        blank(QUERY_PER_KV), scores, mask, value_piece.reshape(count, kv_dev, HEAD_SIZE)
    )
    positions = here * shard + jnp.arange(shard, dtype=jnp.int32)

    def cache_step(carry, q_part, block_id):
        lengths = lax.dynamic_slice_in_dim(all_len, block_id * rows, rows, 0)
        scores = (
            jnp.einsum("rkgd,skd->rkgs", q_part, keys_local, preferred_element_type=jnp.float32)
            * scale
        )
        mask = (positions[None, :] < lengths[:, None])[:, None, None, :]
        return fold_block(carry, scores, mask, vals_local)

    lanes = ((1, 0, QUERY_PER_KV // 2), (-1, QUERY_PER_KV // 2, QUERY_PER_KV))
    lane_queries = tuple((q_heads[:, :, low:high] for way, low, high in lanes))
    own_lanes = tuple((tuple((part[:, :, low:high] for part in own)) for way, low, high in lanes))
    buffers = []
    for n in range(len(lanes)):
        width_g = lanes[n][2] - lanes[n][1]
        first = cache_step(blank(width_g), lane_queries[n], here)
        stacked = tuple((jnp.zeros((cycle,) + part.shape, jnp.float32) for part in first))
        buffers.append(
            tuple(
                (lax.dynamic_update_index_in_dim(stacked[m], first[m], here, 0) for m in range(3))
            )
        )

    def turn(step, loop):
        moving, stored = loop
        new_moving = []
        new_stored = []
        for n in range(len(lanes)):
            way = lanes[n][0]
            width_g = lanes[n][2] - lanes[n][1]
            block_q = move_query(moving[n], way)
            block_id = jnp.mod(here - way * step, cycle)
            result = cache_step(blank(width_g), block_q, block_id)
            new_moving.append(block_q)
            new_stored.append(
                tuple(
                    (
                        lax.dynamic_update_index_in_dim(stored[n][m], result[m], block_id, 0)
                        for m in range(3)
                    )
                )
            )
        return (tuple(new_moving), tuple(new_stored))

    moving, stored = lax.fori_loop(1, cycle, turn, (lane_queries, tuple(buffers)))
    finals = []
    for n in range(len(lanes)):
        got_top, got_total, got_acc = (
            lax.all_to_all(stored[n][0], "ctx", split_axis=0, concat_axis=0, tiled=True),
            lax.all_to_all(stored[n][1], "ctx", split_axis=0, concat_axis=0, tiled=True),
            lax.all_to_all(stored[n][2], "ctx", split_axis=0, concat_axis=0, tiled=True),
        )
        top0, total0, acc0 = own_lanes[n]
        top = jnp.maximum(top0, jnp.max(got_top, axis=0))
        factor0 = jnp.exp(top0 - top)
        factors = jnp.exp(got_top - top[None])
        total = total0 * factor0 + jnp.sum(got_total * factors, axis=0)
        acc = acc0 * factor0[..., None] + jnp.sum(got_acc * factors[..., None], axis=0)
        finals.append((top, total, acc))
    finals = tuple(finals)
    outputs = [state[2] / state[1][..., None] for state in finals]
    attn = (
        jnp.concatenate(outputs, axis=2)
        .astype(jnp.bfloat16)
        .reshape(rows, kv_dev * QUERY_PER_KV * HEAD_SIZE)
    )
    terms = jnp.dot(
        lax.all_gather(attn, "ctx", axis=0, tiled=True),
        out_weight,
        preferred_element_type=jnp.float32,
    )
    return lax.psum_scatter(terms, "kvh", scatter_dimension=0, tiled=True).astype(jnp.bfloat16)


def solution(mesh):
    in_specs = (
        P("ctx", "kvh"),
        P("ctx", "kvh"),
        P("ctx", "kvh"),
        P("ctx", "kvh"),
        P("ctx", "kvh"),
        P("ctx"),
        P("ctx"),
        P("ctx"),
        P("kvh", "ctx"),
    )
    out_specs = P("kvh", "ctx")
    return jax.shard_map(local, mesh=mesh, in_specs=in_specs, out_specs=out_specs, check_vma=False)
```

profile of v0, /device:TPU:1, one launch (start us, length us, event | category | flops | bytes accessed | tf_op | source)
XLA Modules:
  0.0 641.4 jit_solution(7122892583580929665)
XLA Ops:
  12.0 18.9 %all-reduce.3 = (s32[512]{0:T(512)S(1)}, s32[512]{0:T(512)S(1)}, s32[512]{0:T(512)S(1)}) all-reduce(s32[512]{0:T(512)S(1)} %dynamic-update-slice.2, s32[512]{0:T(512)S(1)} %dynamic-update-slice.1, s32[512]{0:T(512)S(1)} %dynamic-update-slice), channel_id=1, replica_groups=mesh['ctx'=32,'kvh'=8] {'ctx'}, use_global_device_ids=true, to_apply=%add.2 | all-reduce | flops 1536 | bytes 12288
  35.6 289.9 %while.30 = (s32[]{:T(128)}, bf16[16,1,4,128]{3,0,2,1:T(8,128)(2,1)S(1)}, bf16[16,1,4,128]{3,0,2,1:T(8,128)(2,1)S(1)}, f32[32,16,1,4]{1,3,2,0:T(4,128)S(1)}, f32...) while((s32[]{:T(128)}, ...), condition=%wide.region_10.11_spmd.clone, body=%wide.region_5.0_spmd.clone.sunk | while | flops 136644640 | bytes 5838663 | solution.py:136
  61.4 6.0 collective-permute-start.1
  80.3 6.0 collective-permute-start.1
  99.1 6.0 collective-permute-start.1
  118.0 6.0 collective-permute-start.1
  127.4 6.0 collective-permute-start.1
  136.9 6.0 collective-permute-start.1
  146.3 6.0 collective-permute-start.1
  155.7 6.0 collective-permute-start.1
  165.2 6.0 collective-permute-start.1
  193.5 6.0 collective-permute-start.1
  202.9 6.0 collective-permute-start.1
  212.3 6.0 collective-permute-start.1
  221.8 6.0 collective-permute-start.1
  231.2 6.0 collective-permute-start.1
  240.6 6.0 collective-permute-start.1
  250.1 6.0 collective-permute-start.1
  259.5 6.0 collective-permute-start.1
  268.9 6.0 collective-permute-start.1
  278.4 6.0 collective-permute-start.1
  297.2 6.0 collective-permute-start.1
  316.1 6.0 collective-permute-start.1
  325.5 19.1 %all_to_all.30 = f32[32,16,1,4]{1,3,2,0:T(4,128)S(1)} all-to-all(f32[32,16,1,4]{1,3,2,0:T(4,128)S(1)} %get-tuple-element.341), channel_id=1, replica_groups=mesh['ctx'=32,'kvh'=8] {'ctx'}, dimensions={0} | all-to-all | bytes 16384 | tf_op jit(solution)/shard_map/all_to_all | solution.py:140
  344.6 12.9 %all_to_all.31 = f32[32,16,1,4]{1,3,2,0:T(4,128)S(1)} all-to-all(f32[32,16,1,4]{1,3,2,0:T(4,128)S(1)} %get-tuple-element.344), channel_id=1, replica_groups=mesh['ctx'=32,'kvh'=8] {'ctx'}, dimensions={0} | all-to-all | bytes 16384 | tf_op jit(solution)/shard_map/all_to_all | solution.py:140
  357.5 12.9 %all_to_all.32 = f32[32,16,1,4]{1,3,2,0:T(4,128)S(1)} all-to-all(f32[32,16,1,4]{1,3,2,0:T(4,128)S(1)} %get-tuple-element.346), channel_id=1, replica_groups=mesh['ctx'=32,'kvh'=8] {'ctx'}, dimensions={0} | all-to-all | bytes 16384 | tf_op jit(solution)/shard_map/all_to_all | solution.py:141
  370.5 12.9 %all_to_all.33 = f32[32,16,1,4]{1,3,2,0:T(4,128)S(1)} all-to-all(f32[32,16,1,4]{1,3,2,0:T(4,128)S(1)} %get-tuple-element.343), channel_id=1, replica_groups=mesh['ctx'=32,'kvh'=8] {'ctx'}, dimensions={0} | all-to-all | bytes 16384 | tf_op jit(solution)/shard_map/all_to_all | solution.py:141
  383.4 32.2 %all_to_all.34 = f32[32,16,1,4,128]{4,1,3,2,0:T(8,128)S(1)} all-to-all(f32[32,16,1,4,128]{4,1,3,2,0:T(8,128)} %get-tuple-element.345), channel_id=1, replica_groups=mesh['ctx'=32,'kvh'=8] {'ctx'}, dimensions={0} | all-to-all | bytes 2097152 | tf_op jit(solution)/shard_map/all_to_all | solution.py:142
  421.6 57.3 %all_gather.20 = bf16[512,128]{1,0:T(8,128)(2,1)S(1)} all-gather(bf16[16,128]{1,0:T(8,128)(2,1)S(1)} %copy-done.6), channel_id=1, replica_groups=mesh['ctx'=32,'kvh'=8] {'ctx'}, dimensions={0}, use_global_device_ids=true | all-gather | bytes 135168 | tf_op jit(solution)/shard_map/all_gather | solution.py:72
  478.9 39.3 %all_gather.21 = bf16[512,128]{1,0:T(8,128)(2,1)S(1)} all-gather(bf16[16,128]{1,0:T(8,128)(2,1)S(1)} %copy-done.7), channel_id=1, replica_groups=mesh['ctx'=32,'kvh'=8] {'ctx'}, dimensions={0}, use_global_device_ids=true | all-gather | bytes 135168 | tf_op jit(solution)/shard_map/all_gather | solution.py:73
  521.0 77.6 %all-gather.2.cloned.1.call-done = bf16[512,1024]{1,0:T(8,128)(2,1)} async-done(((bf16[16,1024]{1,0:T(8,128)(2,1)}), bf16[512,1024]{1,0:T(8,128)(2,1)}) %all-gather.2.cloned.1.call-update) | async-done | bytes 1048592 | tf_op jit(solution)/shard_map/all_gather | solution.py:159
  601.2 31.9 %reduce-scatter.2.cloned.1.call-done = f32[64,256]{1,0:T(8,128)} async-done(((f32[512,256]{1,0:T(8,128)}), f32[64,256]{1,0:T(8,128)}) %reduce-scatter.2.cloned.1.call-update) | async-done | bytes 65552 | tf_op jit(solution)/shard_map/reduce_scatter | solution.py:163
  (650 shorter events, 183.2 us)
Async XLA Ops:
  35.6 7.3 %collective-permute-start.1 = (bf16[16,1,4,128]{3,0,2,1:T(8,128)(2,1)S(1)}, bf16[16,1,4,128]{3,0,2,1:T(8,128)(2,1)S(1)}, u32[]{:S(2)}, u32[]{:S(2)}) collective-permute-start(bf16[16,1,4,128]{3,0,2,1:T(8,128)(2,1)S(1)} %get-tuple-element.581), channel_id=1, source_target_pairs={{8,0},{16,8},{24,16},{32,24},{40,32},{48,40},{56,48},{64,56},{72,6... | collective-permute-start | bytes 49160 | tf_op jit(solution)/shard_map/while/body/eval_jaxpr/ppermute | solution.py:18
  61.4 6.9 %collective-permute-start.1 = (bf16[16,1,4,128]{3,0,2,1:T(8,128)(2,1)S(1)}, bf16[16,1,4,128]{3,0,2,1:T(8,128)(2,1)S(1)}, u32[]{:S(2)}, u32[]{:S(2)}) collective-permute-start(bf16[16,1,4,128]{3,0,2,1:T(8,128)(2,1)S(1)} %get-tuple-element.581), channel_id=1, source_target_pairs={{8,0},{16,8},{24,16},{32,24},{40,32},{48,40},{56,48},{64,56},{72,6... | collective-permute-start | bytes 49160 | tf_op jit(solution)/shard_map/while/body/eval_jaxpr/ppermute | solution.py:18
  70.9 6.8 %collective-permute-start.1 = (bf16[16,1,4,128]{3,0,2,1:T(8,128)(2,1)S(1)}, bf16[16,1,4,128]{3,0,2,1:T(8,128)(2,1)S(1)}, u32[]{:S(2)}, u32[]{:S(2)}) collective-permute-start(bf16[16,1,4,128]{3,0,2,1:T(8,128)(2,1)S(1)} %get-tuple-element.581), channel_id=1, source_target_pairs={{8,0},{16,8},{24,16},{32,24},{40,32},{48,40},{56,48},{64,56},{72,6... | collective-permute-start | bytes 49160 | tf_op jit(solution)/shard_map/while/body/eval_jaxpr/ppermute | solution.py:18
  80.3 6.9 %collective-permute-start.1 = (bf16[16,1,4,128]{3,0,2,1:T(8,128)(2,1)S(1)}, bf16[16,1,4,128]{3,0,2,1:T(8,128)(2,1)S(1)}, u32[]{:S(2)}, u32[]{:S(2)}) collective-permute-start(bf16[16,1,4,128]{3,0,2,1:T(8,128)(2,1)S(1)} %get-tuple-element.581), channel_id=1, source_target_pairs={{8,0},{16,8},{24,16},{32,24},{40,32},{48,40},{56,48},{64,56},{72,6... | collective-permute-start | bytes 49160 | tf_op jit(solution)/shard_map/while/body/eval_jaxpr/ppermute | solution.py:18
  89.7 6.8 %collective-permute-start.1 = (bf16[16,1,4,128]{3,0,2,1:T(8,128)(2,1)S(1)}, bf16[16,1,4,128]{3,0,2,1:T(8,128)(2,1)S(1)}, u32[]{:S(2)}, u32[]{:S(2)}) collective-permute-start(bf16[16,1,4,128]{3,0,2,1:T(8,128)(2,1)S(1)} %get-tuple-element.581), channel_id=1, source_target_pairs={{8,0},{16,8},{24,16},{32,24},{40,32},{48,40},{56,48},{64,56},{72,6... | collective-permute-start | bytes 49160 | tf_op jit(solution)/shard_map/while/body/eval_jaxpr/ppermute | solution.py:18
  99.1 6.9 %collective-permute-start.1 = (bf16[16,1,4,128]{3,0,2,1:T(8,128)(2,1)S(1)}, bf16[16,1,4,128]{3,0,2,1:T(8,128)(2,1)S(1)}, u32[]{:S(2)}, u32[]{:S(2)}) collective-permute-start(bf16[16,1,4,128]{3,0,2,1:T(8,128)(2,1)S(1)} %get-tuple-element.581), channel_id=1, source_target_pairs={{8,0},{16,8},{24,16},{32,24},{40,32},{48,40},{56,48},{64,56},{72,6... | collective-permute-start | bytes 49160 | tf_op jit(solution)/shard_map/while/body/eval_jaxpr/ppermute | solution.py:18
  108.6 6.8 %collective-permute-start.1 = (bf16[16,1,4,128]{3,0,2,1:T(8,128)(2,1)S(1)}, bf16[16,1,4,128]{3,0,2,1:T(8,128)(2,1)S(1)}, u32[]{:S(2)}, u32[]{:S(2)}) collective-permute-start(bf16[16,1,4,128]{3,0,2,1:T(8,128)(2,1)S(1)} %get-tuple-element.581), channel_id=1, source_target_pairs={{8,0},{16,8},{24,16},{32,24},{40,32},{48,40},{56,48},{64,56},{72,6... | collective-permute-start | bytes 49160 | tf_op jit(solution)/shard_map/while/body/eval_jaxpr/ppermute | solution.py:18
  118.0 6.9 %collective-permute-start.1 = (bf16[16,1,4,128]{3,0,2,1:T(8,128)(2,1)S(1)}, bf16[16,1,4,128]{3,0,2,1:T(8,128)(2,1)S(1)}, u32[]{:S(2)}, u32[]{:S(2)}) collective-permute-start(bf16[16,1,4,128]{3,0,2,1:T(8,128)(2,1)S(1)} %get-tuple-element.581), channel_id=1, source_target_pairs={{8,0},{16,8},{24,16},{32,24},{40,32},{48,40},{56,48},{64,56},{72,6... | collective-permute-start | bytes 49160 | tf_op jit(solution)/shard_map/while/body/eval_jaxpr/ppermute | solution.py:18
  127.4 6.9 %collective-permute-start.1 = (bf16[16,1,4,128]{3,0,2,1:T(8,128)(2,1)S(1)}, bf16[16,1,4,128]{3,0,2,1:T(8,128)(2,1)S(1)}, u32[]{:S(2)}, u32[]{:S(2)}) collective-permute-start(bf16[16,1,4,128]{3,0,2,1:T(8,128)(2,1)S(1)} %get-tuple-element.581), channel_id=1, source_target_pairs={{8,0},{16,8},{24,16},{32,24},{40,32},{48,40},{56,48},{64,56},{72,6... | collective-permute-start | bytes 49160 | tf_op jit(solution)/shard_map/while/body/eval_jaxpr/ppermute | solution.py:18
  136.9 6.9 %collective-permute-start.1 = (bf16[16,1,4,128]{3,0,2,1:T(8,128)(2,1)S(1)}, bf16[16,1,4,128]{3,0,2,1:T(8,128)(2,1)S(1)}, u32[]{:S(2)}, u32[]{:S(2)}) collective-permute-start(bf16[16,1,4,128]{3,0,2,1:T(8,128)(2,1)S(1)} %get-tuple-element.581), channel_id=1, source_target_pairs={{8,0},{16,8},{24,16},{32,24},{40,32},{48,40},{56,48},{64,56},{72,6... | collective-permute-start | bytes 49160 | tf_op jit(solution)/shard_map/while/body/eval_jaxpr/ppermute | solution.py:18
  146.3 6.9 %collective-permute-start.1 = (bf16[16,1,4,128]{3,0,2,1:T(8,128)(2,1)S(1)}, bf16[16,1,4,128]{3,0,2,1:T(8,128)(2,1)S(1)}, u32[]{:S(2)}, u32[]{:S(2)}) collective-permute-start(bf16[16,1,4,128]{3,0,2,1:T(8,128)(2,1)S(1)} %get-tuple-element.581), channel_id=1, source_target_pairs={{8,0},{16,8},{24,16},{32,24},{40,32},{48,40},{56,48},{64,56},{72,6... | collective-permute-start | bytes 49160 | tf_op jit(solution)/shard_map/while/body/eval_jaxpr/ppermute | solution.py:18
  155.7 6.9 %collective-permute-start.1 = (bf16[16,1,4,128]{3,0,2,1:T(8,128)(2,1)S(1)}, bf16[16,1,4,128]{3,0,2,1:T(8,128)(2,1)S(1)}, u32[]{:S(2)}, u32[]{:S(2)}) collective-permute-start(bf16[16,1,4,128]{3,0,2,1:T(8,128)(2,1)S(1)} %get-tuple-element.581), channel_id=1, source_target_pairs={{8,0},{16,8},{24,16},{32,24},{40,32},{48,40},{56,48},{64,56},{72,6... | collective-permute-start | bytes 49160 | tf_op jit(solution)/shard_map/while/body/eval_jaxpr/ppermute | solution.py:18
  165.2 6.9 %collective-permute-start.1 = (bf16[16,1,4,128]{3,0,2,1:T(8,128)(2,1)S(1)}, bf16[16,1,4,128]{3,0,2,1:T(8,128)(2,1)S(1)}, u32[]{:S(2)}, u32[]{:S(2)}) collective-permute-start(bf16[16,1,4,128]{3,0,2,1:T(8,128)(2,1)S(1)} %get-tuple-element.581), channel_id=1, source_target_pairs={{8,0},{16,8},{24,16},{32,24},{40,32},{48,40},{56,48},{64,56},{72,6... | collective-permute-start | bytes 49160 | tf_op jit(solution)/shard_map/while/body/eval_jaxpr/ppermute | solution.py:18
  174.6 6.8 %collective-permute-start.1 = (bf16[16,1,4,128]{3,0,2,1:T(8,128)(2,1)S(1)}, bf16[16,1,4,128]{3,0,2,1:T(8,128)(2,1)S(1)}, u32[]{:S(2)}, u32[]{:S(2)}) collective-permute-start(bf16[16,1,4,128]{3,0,2,1:T(8,128)(2,1)S(1)} %get-tuple-element.581), channel_id=1, source_target_pairs={{8,0},{16,8},{24,16},{32,24},{40,32},{48,40},{56,48},{64,56},{72,6... | collective-permute-start | bytes 49160 | tf_op jit(solution)/shard_map/while/body/eval_jaxpr/ppermute | solution.py:18
  184.0 6.8 %collective-permute-start.1 = (bf16[16,1,4,128]{3,0,2,1:T(8,128)(2,1)S(1)}, bf16[16,1,4,128]{3,0,2,1:T(8,128)(2,1)S(1)}, u32[]{:S(2)}, u32[]{:S(2)}) collective-permute-start(bf16[16,1,4,128]{3,0,2,1:T(8,128)(2,1)S(1)} %get-tuple-element.581), channel_id=1, source_target_pairs={{8,0},{16,8},{24,16},{32,24},{40,32},{48,40},{56,48},{64,56},{72,6... | collective-permute-start | bytes 49160 | tf_op jit(solution)/shard_map/while/body/eval_jaxpr/ppermute | solution.py:18
  193.5 6.9 %collective-permute-start.1 = (bf16[16,1,4,128]{3,0,2,1:T(8,128)(2,1)S(1)}, bf16[16,1,4,128]{3,0,2,1:T(8,128)(2,1)S(1)}, u32[]{:S(2)}, u32[]{:S(2)}) collective-permute-start(bf16[16,1,4,128]{3,0,2,1:T(8,128)(2,1)S(1)} %get-tuple-element.581), channel_id=1, source_target_pairs={{8,0},{16,8},{24,16},{32,24},{40,32},{48,40},{56,48},{64,56},{72,6... | collective-permute-start | bytes 49160 | tf_op jit(solution)/shard_map/while/body/eval_jaxpr/ppermute | solution.py:18
  202.9 6.9 %collective-permute-start.1 = (bf16[16,1,4,128]{3,0,2,1:T(8,128)(2,1)S(1)}, bf16[16,1,4,128]{3,0,2,1:T(8,128)(2,1)S(1)}, u32[]{:S(2)}, u32[]{:S(2)}) collective-permute-start(bf16[16,1,4,128]{3,0,2,1:T(8,128)(2,1)S(1)} %get-tuple-element.581), channel_id=1, source_target_pairs={{8,0},{16,8},{24,16},{32,24},{40,32},{48,40},{56,48},{64,56},{72,6... | collective-permute-start | bytes 49160 | tf_op jit(solution)/shard_map/while/body/eval_jaxpr/ppermute | solution.py:18
  212.3 6.9 %collective-permute-start.1 = (bf16[16,1,4,128]{3,0,2,1:T(8,128)(2,1)S(1)}, bf16[16,1,4,128]{3,0,2,1:T(8,128)(2,1)S(1)}, u32[]{:S(2)}, u32[]{:S(2)}) collective-permute-start(bf16[16,1,4,128]{3,0,2,1:T(8,128)(2,1)S(1)} %get-tuple-element.581), channel_id=1, source_target_pairs={{8,0},{16,8},{24,16},{32,24},{40,32},{48,40},{56,48},{64,56},{72,6... | collective-permute-start | bytes 49160 | tf_op jit(solution)/shard_map/while/body/eval_jaxpr/ppermute | solution.py:18
  221.8 6.9 %collective-permute-start.1 = (bf16[16,1,4,128]{3,0,2,1:T(8,128)(2,1)S(1)}, bf16[16,1,4,128]{3,0,2,1:T(8,128)(2,1)S(1)}, u32[]{:S(2)}, u32[]{:S(2)}) collective-permute-start(bf16[16,1,4,128]{3,0,2,1:T(8,128)(2,1)S(1)} %get-tuple-element.581), channel_id=1, source_target_pairs={{8,0},{16,8},{24,16},{32,24},{40,32},{48,40},{56,48},{64,56},{72,6... | collective-permute-start | bytes 49160 | tf_op jit(solution)/shard_map/while/body/eval_jaxpr/ppermute | solution.py:18
  231.2 6.9 %collective-permute-start.1 = (bf16[16,1,4,128]{3,0,2,1:T(8,128)(2,1)S(1)}, bf16[16,1,4,128]{3,0,2,1:T(8,128)(2,1)S(1)}, u32[]{:S(2)}, u32[]{:S(2)}) collective-permute-start(bf16[16,1,4,128]{3,0,2,1:T(8,128)(2,1)S(1)} %get-tuple-element.581), channel_id=1, source_target_pairs={{8,0},{16,8},{24,16},{32,24},{40,32},{48,40},{56,48},{64,56},{72,6... | collective-permute-start | bytes 49160 | tf_op jit(solution)/shard_map/while/body/eval_jaxpr/ppermute | solution.py:18
  240.6 6.9 %collective-permute-start.1 = (bf16[16,1,4,128]{3,0,2,1:T(8,128)(2,1)S(1)}, bf16[16,1,4,128]{3,0,2,1:T(8,128)(2,1)S(1)}, u32[]{:S(2)}, u32[]{:S(2)}) collective-permute-start(bf16[16,1,4,128]{3,0,2,1:T(8,128)(2,1)S(1)} %get-tuple-element.581), channel_id=1, source_target_pairs={{8,0},{16,8},{24,16},{32,24},{40,32},{48,40},{56,48},{64,56},{72,6... | collective-permute-start | bytes 49160 | tf_op jit(solution)/shard_map/while/body/eval_jaxpr/ppermute | solution.py:18
  250.1 6.9 %collective-permute-start.1 = (bf16[16,1,4,128]{3,0,2,1:T(8,128)(2,1)S(1)}, bf16[16,1,4,128]{3,0,2,1:T(8,128)(2,1)S(1)}, u32[]{:S(2)}, u32[]{:S(2)}) collective-permute-start(bf16[16,1,4,128]{3,0,2,1:T(8,128)(2,1)S(1)} %get-tuple-element.581), channel_id=1, source_target_pairs={{8,0},{16,8},{24,16},{32,24},{40,32},{48,40},{56,48},{64,56},{72,6... | collective-permute-start | bytes 49160 | tf_op jit(solution)/shard_map/while/body/eval_jaxpr/ppermute | solution.py:18
  259.5 6.9 %collective-permute-start.1 = (bf16[16,1,4,128]{3,0,2,1:T(8,128)(2,1)S(1)}, bf16[16,1,4,128]{3,0,2,1:T(8,128)(2,1)S(1)}, u32[]{:S(2)}, u32[]{:S(2)}) collective-permute-start(bf16[16,1,4,128]{3,0,2,1:T(8,128)(2,1)S(1)} %get-tuple-element.581), channel_id=1, source_target_pairs={{8,0},{16,8},{24,16},{32,24},{40,32},{48,40},{56,48},{64,56},{72,6... | collective-permute-start | bytes 49160 | tf_op jit(solution)/shard_map/while/body/eval_jaxpr/ppermute | solution.py:18
  268.9 6.9 %collective-permute-start.1 = (bf16[16,1,4,128]{3,0,2,1:T(8,128)(2,1)S(1)}, bf16[16,1,4,128]{3,0,2,1:T(8,128)(2,1)S(1)}, u32[]{:S(2)}, u32[]{:S(2)}) collective-permute-start(bf16[16,1,4,128]{3,0,2,1:T(8,128)(2,1)S(1)} %get-tuple-element.581), channel_id=1, source_target_pairs={{8,0},{16,8},{24,16},{32,24},{40,32},{48,40},{56,48},{64,56},{72,6... | collective-permute-start | bytes 49160 | tf_op jit(solution)/shard_map/while/body/eval_jaxpr/ppermute | solution.py:18
  278.4 6.9 %collective-permute-start.1 = (bf16[16,1,4,128]{3,0,2,1:T(8,128)(2,1)S(1)}, bf16[16,1,4,128]{3,0,2,1:T(8,128)(2,1)S(1)}, u32[]{:S(2)}, u32[]{:S(2)}) collective-permute-start(bf16[16,1,4,128]{3,0,2,1:T(8,128)(2,1)S(1)} %get-tuple-element.581), channel_id=1, source_target_pairs={{8,0},{16,8},{24,16},{32,24},{40,32},{48,40},{56,48},{64,56},{72,6... | collective-permute-start | bytes 49160 | tf_op jit(solution)/shard_map/while/body/eval_jaxpr/ppermute | solution.py:18
  287.8 6.8 %collective-permute-start.1 = (bf16[16,1,4,128]{3,0,2,1:T(8,128)(2,1)S(1)}, bf16[16,1,4,128]{3,0,2,1:T(8,128)(2,1)S(1)}, u32[]{:S(2)}, u32[]{:S(2)}) collective-permute-start(bf16[16,1,4,128]{3,0,2,1:T(8,128)(2,1)S(1)} %get-tuple-element.581), channel_id=1, source_target_pairs={{8,0},{16,8},{24,16},{32,24},{40,32},{48,40},{56,48},{64,56},{72,6... | collective-permute-start | bytes 49160 | tf_op jit(solution)/shard_map/while/body/eval_jaxpr/ppermute | solution.py:18
  297.2 6.9 %collective-permute-start.1 = (bf16[16,1,4,128]{3,0,2,1:T(8,128)(2,1)S(1)}, bf16[16,1,4,128]{3,0,2,1:T(8,128)(2,1)S(1)}, u32[]{:S(2)}, u32[]{:S(2)}) collective-permute-start(bf16[16,1,4,128]{3,0,2,1:T(8,128)(2,1)S(1)} %get-tuple-element.581), channel_id=1, source_target_pairs={{8,0},{16,8},{24,16},{32,24},{40,32},{48,40},{56,48},{64,56},{72,6... | collective-permute-start | bytes 49160 | tf_op jit(solution)/shard_map/while/body/eval_jaxpr/ppermute | solution.py:18
  306.7 6.8 %collective-permute-start.1 = (bf16[16,1,4,128]{3,0,2,1:T(8,128)(2,1)S(1)}, bf16[16,1,4,128]{3,0,2,1:T(8,128)(2,1)S(1)}, u32[]{:S(2)}, u32[]{:S(2)}) collective-permute-start(bf16[16,1,4,128]{3,0,2,1:T(8,128)(2,1)S(1)} %get-tuple-element.581), channel_id=1, source_target_pairs={{8,0},{16,8},{24,16},{32,24},{40,32},{48,40},{56,48},{64,56},{72,6... | collective-permute-start | bytes 49160 | tf_op jit(solution)/shard_map/while/body/eval_jaxpr/ppermute | solution.py:18
  316.1 6.9 %collective-permute-start.1 = (bf16[16,1,4,128]{3,0,2,1:T(8,128)(2,1)S(1)}, bf16[16,1,4,128]{3,0,2,1:T(8,128)(2,1)S(1)}, u32[]{:S(2)}, u32[]{:S(2)}) collective-permute-start(bf16[16,1,4,128]{3,0,2,1:T(8,128)(2,1)S(1)} %get-tuple-element.581), channel_id=1, source_target_pairs={{8,0},{16,8},{24,16},{32,24},{40,32},{48,40},{56,48},{64,56},{72,6... | collective-permute-start | bytes 49160 | tf_op jit(solution)/shard_map/while/body/eval_jaxpr/ppermute | solution.py:18
  415.5 104.3 %all-to-all-start.1 = ((f32[32,16,1,4,128]{4,1,3,2,0:T(8,128)}), f32[32,16,1,4,128]{4,1,3,2,0:T(8,128)S(1)}, u32[]{:S(2)}, u32[]{:S(2)}) async-start(f32[32,16,1,4,128]{4,1,3,2,0:T(8,128)} %copy-done.3), calls=%async_computation.1 | async-start | bytes 2097152 | tf_op jit(solution)/shard_map/all_to_all | solution.py:142
  421.5 177.1 %all-gather.2.cloned.1.call-start = ((), (), s32[]{:S(2)}) async-start(), calls=%async_computation.7 | async-start | bytes 1081344 | tf_op jit(solution)/shard_map/all_gather | solution.py:159
  521.0 112.1 %reduce-scatter.2.cloned.1.call-start = ((), (), s32[]{:S(2)}) async-start(), calls=%async_computation.8 | async-start | bytes 589824 | tf_op jit(solution)/shard_map/reduce_scatter | solution.py:163
  (45 other events, 804.9 us)
Sparse Core Ops, SparseCore 0:
  521.1 77.5 all-gather.1
  601.3 31.7 reduce-scatter.1
where the time goes:
time: 646 us; the launch traced here: 641 us
  blocking collectives  205 us (32%)
  starting transfers between devices  189 us (29%)
  waiting for transfers between devices  130 us (20%)
  matrix products  67 us (10%)
  other arithmetic  23 us (4%)
  between operations  14.4 us (2%)
  local copies, waits for them, and re-layouts  9.93 us (2%)
    ppermute x62, starting transfers between devices, passed_along(): return lax.ppermute(block, axis, route)  183 us
    all_gather x1, waiting for transfers between devices, local(): lax.all_gather(attn, 'ctx', axis=0, tiled=True)  77.6 us
    all_gather x1, blocking collectives, local(): key_piece = lax.all_gather(candidate_row_keys, 'ctx', axis=0, tiled=True)  57.3 us
    all_gather x1, blocking collectives, local(): value_piece = lax.all_gather(candidate_values, 'ctx', axis=0, tiled=True)  39.3 us
    dot_general x65, matrix products, fold_block(): jnp.einsum('rkgn,nkd->rkgd', probs.astype(jnp.bfloat16), values, preferre...  38.7 us
    all_to_all x1, blocking collectives, local(): lax.all_to_all(stored[n][2], 'ctx', split_axis=0, concat_axis=0, tiled=True)  32.2 us
    all_to_all x2, blocking collectives, local(): lax.all_to_all(stored[n][0], 'ctx', split_axis=0, concat_axis=0, tiled=True)  32 us
    reduce_scatter x1, waiting for transfers between devices, local(): lax.psum_scatter(terms, 'kvh', scatter_dimension=0, tiled=True)  31.9 us
  transfers between devices with their start and end apart: 65, of which 33 were waited for; matrix products, arithmetic and copies ran while one was open for 3% of the time, Pallas kernels for 0%

commit v1 on v0

v1 whole, which is shorter than its diff:
```python
import math

import jax
import jax.numpy as jnp
from jax import lax
from jax.experimental import pallas as pl
from jax.experimental.pallas import tpu as pltpu
from jax.sharding import PartitionSpec as P

MESH = pl.DeviceIdType.MESH
BF = jnp.bfloat16
F32 = jnp.float32
HEAD = 128
HEADS = 8
ROWS = 16
RINGZ = 8
SHARD = 2048
PAIR = 2 * SHARD
CAND = 2 * ROWS
KPOS = PAIR + CAND
VPOS = PAIR + 128
QH = HEADS * ROWS
QW = HEADS * HEAD + 128
BLK = HEAD + 16
COLS = 256
NEG = -1e30
SCALE = math.log2(math.e) / math.sqrt(HEAD)
CQ = 256
CP = 1024


def split2(x):
    hi = x.astype(BF)
    lo = (x - hi.astype(F32)).astype(BF)
    return hi, lo


def kernel(
    q_hbm, k_hbm, v_hbm, ck_hbm, cv_hbm, len_s, branch_s, depth_s, w_hbm,
    out_ref,
    qall, kbuf, vraw, vt, cvraw, cinfo, wbuf, sa, sb, pbuf, ma, mb, part, got, blk, attn, prod, terms,
    loc, kv_s, kv_r, q_s, q_r, p_s, p_r, a_s, a_r, t_s, t_r,
):
    ctx = lax.axis_index("ctx")
    kvh = lax.axis_index("kvh")
    z = ctx // 4
    yh = (ctx // 2) % 2
    core = ctx % 2

    def plane(dz, so):
        zz = (z + dz) % RINGZ
        yy = (yh + so) % 2
        return (zz * 4 + yy * 2 + core, kvh)

    sibling = (ctx + 1 - 2 * core, kvh)

    def head_group(k, c):
        return (ctx - core + c, k)

    bar = pltpu.get_barrier_semaphore()
    for dz in range(RINGZ):
        for so in range(2):
            if dz or so:
                pl.semaphore_signal(bar, inc=1, device_id=plane(dz, so), device_id_type=MESH)
    pl.semaphore_signal(bar, inc=1, device_id=sibling, device_id_type=MESH)
    for dk in range(1, RINGZ):
        for c in range(2):
            pl.semaphore_signal(
                bar, inc=1, device_id=head_group((kvh + dk) % RINGZ, c), device_id_type=MESH
            )

    mine = pl.multiple_of(core * SHARD, SHARD)
    cmine = pl.multiple_of(PAIR + core * ROWS, ROWS)
    crow = pl.multiple_of(core * ROWS, ROWS)
    wmine = pl.multiple_of(core * COLS, COLS)
    loads = [
        pltpu.make_async_copy(q_hbm, qall.at[0, 0, :, pl.ds(0, HEADS * HEAD)], loc.at[0]),
        pltpu.make_async_copy(k_hbm, kbuf.at[pl.ds(mine, SHARD)], loc.at[1]),
        pltpu.make_async_copy(v_hbm, vraw, loc.at[2]),
        pltpu.make_async_copy(ck_hbm, kbuf.at[pl.ds(cmine, ROWS)], loc.at[3]),
        pltpu.make_async_copy(cv_hbm, cvraw.at[pl.ds(crow, ROWS)], loc.at[4]),
        pltpu.make_async_copy(w_hbm, wbuf.at[:, pl.ds(wmine, COLS)], loc.at[5]),
    ]
    for copy in loads:
        copy.start()

    lane = lax.broadcasted_iota(jnp.int32, (ROWS, QH), 1)
    sub = lax.broadcasted_iota(jnp.int32, (ROWS, QH), 0)
    lane_row = lane % ROWS
    meta = jnp.zeros((ROWS, QH), jnp.int32)
    cb = jnp.zeros((ROWS, QH), jnp.int32)
    cd = jnp.zeros((ROWS, QH), jnp.int32)
    for i in range(ROWS):
        n = len_s[i]
        b = branch_s[i]
        d = depth_s[i]
        high = n // 256
        col = jnp.where(
            sub == 0, high, jnp.where(sub == 1, n - high * 256, jnp.where(sub == 2, b, d))
        )
        meta = jnp.where(lane_row == i, col, meta)
        cb = jnp.where(sub == i, b, cb)
        cd = jnp.where(sub == i, d, cd)
    qall[0, 0, :, HEADS * HEAD :] = meta.astype(F32).astype(BF)
    cinfo[core, 0] = cb.astype(F32).astype(BF)
    cinfo[core, 1] = cd.astype(F32).astype(BF)
    pbuf[KPOS:, :] = jnp.zeros((VPOS - KPOS, 2 * QH), BF)
    vt[HEAD:, :] = jnp.ones((BLK - HEAD, VPOS), BF)
    cvraw[CAND:, :] = jnp.zeros((128 - CAND, HEAD), BF)
    for copy in loads:
        copy.wait()
    for j in range(0, SHARD, 128):
        vt[0:HEAD, pl.ds(pl.multiple_of(mine + j, 128), 128)] = vraw[j : j + 128, :].T

    pl.semaphore_wait(bar, 30)

    def swap(n, ref):
        return pltpu.make_async_remote_copy(
            src_ref=ref, dst_ref=ref, send_sem=kv_s.at[n], recv_sem=kv_r.at[n],
            device_id=sibling, device_id_type=MESH,
        )

    def swaps(side):
        base = pl.multiple_of(side * SHARD, SHARD)
        cbase = pl.multiple_of(PAIR + side * ROWS, ROWS)
        rbase = pl.multiple_of(side * ROWS, ROWS)
        wbase = pl.multiple_of(side * COLS, COLS)
        return [
            swap(0, kbuf.at[pl.ds(base, SHARD)]),
            swap(1, kbuf.at[pl.ds(cbase, ROWS)]),
            swap(2, cvraw.at[pl.ds(rbase, ROWS)]),
            swap(3, cinfo.at[side]),
            swap(4, vt.at[pl.ds(0, HEAD), pl.ds(base, SHARD)]),
            swap(5, wbuf.at[:, pl.ds(wbase, COLS)]),
        ]

    def around(dz, so, src, dst, send, recv):
        back = (RINGZ - dz) % RINGZ
        return pltpu.make_async_remote_copy(
            src_ref=src, dst_ref=dst.at[back, so], send_sem=send.at[dz * 2 + so],
            recv_sem=recv.at[back * 2 + so], device_id=plane(dz, so), device_id_type=MESH,
        )

    def arrival(dz, so, dst, recv):
        return pltpu.make_async_remote_copy(
            src_ref=dst.at[dz, so], dst_ref=dst.at[dz, so], send_sem=recv.at[dz * 2 + so],
            recv_sem=recv.at[dz * 2 + so], device_id=plane(dz, so), device_id_type=MESH,
        )

    order = [1, 7, 2, 6, 3, 5, 4, 0]
    q_out = []
    for dz in order:
        for so in range(2):
            if dz or so:
                copy = around(dz, so, qall.at[0, 0], qall, q_s, q_r)
                copy.start()
                q_out.append(copy)
    out_swaps = swaps(core)
    in_swaps = swaps(1 - core)
    for copy in out_swaps:
        copy.start()
    for n in range(4):
        in_swaps[n].wait_recv()

    base = (ctx - core) * SHARD
    pos_sub = lax.broadcasted_iota(jnp.int32, (CQ, QH), 0)

    def offset(t):
        return (((t // 2) + 1) * (1 - 2 * (t % 2)) + RINGZ) % RINGZ

    def load_q(dz):
        parts = []
        infos = []
        for so in range(2):
            for h in range(HEADS):
                parts.append(qall[dz, so, :, h * HEAD : (h + 1) * HEAD])
            infos.append(qall[dz, so, :, HEADS * HEAD :].astype(F32))
        q = jnp.concatenate(parts, axis=0).astype(F32) * SCALE
        hi, lo = split2(q)
        lens = [(f[0:1] * 256.0 + f[1:2]).astype(jnp.int32) - base for f in infos]
        return jnp.concatenate([hi, lo], axis=1), lens, infos

    def score(q, pos, width):
        k = kbuf[pos : pos + width, :]
        return lax.dot_general(
            jnp.concatenate([k, k], axis=1), q, (((1,), (1,)), ((), ())),
            preferred_element_type=F32,
        )

    def fused(dz_new, dz_old, parity):
        s_new, s_old = (sa, sb) if parity == 0 else (sb, sa)
        m_new, m_old = (ma, mb) if parity == 0 else (mb, ma)
        if dz_new is not None:
            q, lens, infos = load_q(dz_new)
            top = jnp.full((8, 2 * QH), NEG, F32)
            s = score(q, PAIR, CAND)
            cbr = jnp.concatenate([cinfo[0, 0], cinfo[1, 0]], axis=0).astype(F32)
            cde = jnp.concatenate([cinfo[0, 1], cinfo[1, 1]], axis=0).astype(F32)
            s = jnp.concatenate(
                [
                    jnp.where(
                        (cbr == f[2:3]) & (cde <= f[3:4]), s[:, n * QH : (n + 1) * QH], NEG
                    )
                    for n, f in enumerate(infos)
                ],
                axis=1,
            )
            s_new[PAIR:KPOS, :] = s
            for j in range(0, CAND, 8):
                top = jnp.maximum(top, s[j : j + 8, :])
        if dz_old is not None:
            m = m_old[0:1, :]
            acc = None
            start = 0
        for pos in range(0, PAIR, CQ):
            if dz_new is not None:
                s = score(q, pos, CQ)
                s = jnp.concatenate(
                    [
                        jnp.where(pos_sub < n - pos, s[:, j * QH : (j + 1) * QH], NEG)
                        for j, n in enumerate(lens)
                    ],
                    axis=1,
                )
                s_new[pos : pos + CQ, :] = s
                for j in range(0, CQ, 8):
                    top = jnp.maximum(top, s[j : j + 8, :])
            if dz_old is not None:
                pbuf[pos : pos + CQ, :] = jnp.exp2(s_old[pos : pos + CQ, :] - m).astype(BF)
                end = pos + CQ
                if end == PAIR:
                    pbuf[PAIR:KPOS, :] = jnp.exp2(s_old[PAIR:KPOS, :] - m).astype(BF)
                    end = VPOS
                if end - start >= CP:
                    term = jnp.dot(
                        vt[:, start:end], pbuf[start:end, :], preferred_element_type=F32
                    )
                    acc = term if acc is None else acc + term
                    start = end
        if dz_old is not None:
            total = acc[HEAD : HEAD + 1]
            m_hi, rest = m.astype(BF), m - m.astype(BF).astype(F32)
            m_mid, m_lo = split2(rest)
            l_hi, l_lo = split2(total)
            row = lax.broadcasted_iota(jnp.int32, (BLK - HEAD, 2 * QH), 0)
            stats = jnp.zeros((BLK - HEAD, 2 * QH), F32)
            for n, x in enumerate((m_hi, m_mid, m_lo, l_hi, l_lo)):
                stats = jnp.where(row == n, x.astype(F32), stats)
            for so in range(2):
                lanes = slice(so * QH, (so + 1) * QH)
                part[dz_old, so, 0:HEAD, :] = acc[0:HEAD, lanes].astype(BF)
                part[dz_old, so, HEAD:, :] = stats[:, lanes].astype(BF)
        if dz_new is not None:
            m_new[...] = jnp.broadcast_to(jnp.max(top, axis=0, keepdims=True), (8, 2 * QH))

    def send_part(dz):
        back = (RINGZ - dz) % RINGZ
        for so in range(2):
            pltpu.make_async_remote_copy(
                src_ref=part.at[dz, so], dst_ref=got.at[back, so], send_sem=p_s.at[dz * 2 + so],
                recv_sem=p_r.at[back * 2 + so], device_id=plane(dz, so), device_id_type=MESH,
            ).start()

    def arrive_q(dz):
        for so in range(2):
            arrival(dz, so, qall, q_r).wait_recv()

    arrive_q(1)
    fused(1, None, 0)
    in_swaps[4].wait_recv()
    vt[0:HEAD, PAIR:] = cvraw[...].T

    def body(i, carry):
        a, b, c = offset(2 * i), offset(2 * i + 1), offset(2 * i + 2)
        arrive_q(b)
        fused(b, a, 1)
        send_part(a)
        arrive_q(c)
        fused(c, b, 0)
        send_part(b)
        return carry

    lax.fori_loop(0, 3, body, 0)
    arrival(0, 1, qall, q_r).wait_recv()
    fused(0, 4, 1)
    send_part(4)
    fused(None, 0, 0)
    other = around(0, 1, part.at[0, 1], got, p_s, p_r)
    other.start()
    got[0, 0] = part[0, 0]

    for dz in range(RINGZ):
        for so in range(2):
            if dz or so:
                arrival(dz, so, got, p_r).wait_recv()
    tops = []
    totals = []
    for dz in range(RINGZ):
        for so in range(2):
            st = got[dz, so, HEAD:, :].astype(F32)
            tops.append(st[0:1] + st[1:2] + st[2:3])
            totals.append(st[3:4] + st[4:5])
    top = tops[0]
    for x in tops[1:]:
        top = jnp.maximum(top, x)
    acc = jnp.zeros((HEAD, QH), F32)
    total = jnp.zeros((1, QH), F32)
    for n in range(2 * RINGZ):
        f = jnp.exp2(tops[n] - top)
        total = total + totals[n] * f
        acc = acc + got[n // 2, n % 2, 0:HEAD, :].astype(F32) * f
    own = (acc / total).T.astype(BF)
    for h in range(HEADS):
        blk[:, h * HEAD : (h + 1) * HEAD] = own[h * ROWS : (h + 1) * ROWS, :]
    a_out = []
    for dz in (4, 3, 5, 2, 6, 1, 7, 0):
        for so in range(2):
            if dz or so:
                copy = around(dz, so, blk, attn, a_s, a_r)
                copy.start()
                a_out.append(copy)
    attn[0, 0] = blk[...]

    in_swaps[5].wait_recv()
    me = kvh * 2 + core

    def term_copy(n, k, c):
        return pltpu.make_async_remote_copy(
            src_ref=prod.at[n, c], dst_ref=terms.at[me], send_sem=t_s.at[n * 2 + c],
            recv_sem=t_r.at[me], device_id=head_group(k, c), device_id_type=MESH,
        )

    for n in (0, 1, 7, 2, 6, 3, 5, 4):
        for so in range(2):
            if n or so:
                arrival(n, so, attn, a_r).wait_recv()
        rows = jnp.concatenate([attn[n, 0], attn[n, 1]], axis=0)
        res = jnp.dot(rows, wbuf[...], preferred_element_type=F32).astype(BF)
        k = (z + n) % RINGZ
        for c in range(2):
            prod[n, c] = res[:, c * COLS : (c + 1) * COLS]
        for c in range(2):
            here = (k == kvh) & (core == c)

            @pl.when(here)
            def _():
                terms[me] = prod[n, c]

            @pl.when(jnp.logical_not(here))
            def _():
                term_copy(n, k, c).start()

    for k in range(RINGZ):
        for c in range(2):
            idx = k * 2 + c

            @pl.when(idx != me)
            def _():
                pltpu.make_async_remote_copy(
                    src_ref=terms.at[idx], dst_ref=terms.at[idx], send_sem=t_r.at[idx],
                    recv_sem=t_r.at[idx], device_id=sibling, device_id_type=MESH,
                ).wait_recv()

    for c in range(2):
        res = terms[c].astype(F32)
        for k in range(1, RINGZ):
            res = res + terms[k * 2 + c].astype(F32)
        res = res.astype(BF)
        for so in range(2):
            row = pl.multiple_of(((yh + so) % 2) * CAND + c * ROWS, ROWS)
            out_ref[pl.ds(row, ROWS), :] = res[so * ROWS : (so + 1) * ROWS, :]

    for copy in q_out + out_swaps + a_out:
        copy.wait_send()
    for dz in range(RINGZ):
        for so in range(2):
            if dz or so:
                around(dz, so, part.at[dz, so], got, p_s, p_r).wait_send()
    for n in range(RINGZ):
        k = (z + n) % RINGZ
        for c in range(2):

            @pl.when(jnp.logical_not((k == kvh) & (core == c)))
            def _():
                term_copy(n, k, c).wait_send()


def local(q, k, v, ck, cv, length, branch, depth, w):
    hbm = pl.BlockSpec(memory_space=pl.ANY)
    smem = pl.BlockSpec(memory_space=pltpu.SMEM)
    dma = pltpu.SemaphoreType.DMA
    return pl.pallas_call(
        kernel,
        out_shape=jax.ShapeDtypeStruct((4 * ROWS, COLS), BF),
        in_specs=[hbm] * 5 + [smem] * 3 + [hbm],
        out_specs=pl.BlockSpec(memory_space=pltpu.VMEM),
        scratch_shapes=[
            pltpu.VMEM((RINGZ, 2, ROWS, QW), BF),
            pltpu.VMEM((KPOS, HEAD), BF),
            pltpu.VMEM((SHARD, HEAD), BF),
            pltpu.VMEM((BLK, VPOS), BF),
            pltpu.VMEM((128, HEAD), BF),
            pltpu.VMEM((2, 2, ROWS, QH), BF),
            pltpu.VMEM((HEADS * HEAD, 2 * COLS), BF),
            pltpu.VMEM((KPOS, 2 * QH), F32),
            pltpu.VMEM((KPOS, 2 * QH), F32),
            pltpu.VMEM((VPOS, 2 * QH), BF),
            pltpu.VMEM((8, 2 * QH), F32),
            pltpu.VMEM((8, 2 * QH), F32),
            pltpu.VMEM((RINGZ, 2, BLK, QH), BF),
            pltpu.VMEM((RINGZ, 2, BLK, QH), BF),
            pltpu.VMEM((ROWS, HEADS * HEAD), BF),
            pltpu.VMEM((RINGZ, 2, ROWS, HEADS * HEAD), BF),
            pltpu.VMEM((RINGZ, 2, 2 * ROWS, COLS), BF),
            pltpu.VMEM((2 * RINGZ, 2 * ROWS, COLS), BF),
            dma((6,)), dma((6,)), dma((6,)),
            dma((16,)), dma((16,)), dma((16,)), dma((16,)),
            dma((16,)), dma((16,)), dma((16,)), dma((16,)),
        ],
        compiler_params=pltpu.CompilerParams(
            collective_id=0, has_side_effects=True, vmem_limit_bytes=48 * 2**20
        ),
        cost_estimate=pl.CostEstimate(
            flops=9 * 10**9, bytes_accessed=2 * 2**20, transcendentals=2048 * 4224
        ),
    )(q, k, v, ck, cv, length, branch, depth, w)


def solution(mesh):
    in_specs = (
        P("ctx", "kvh"),
        P("ctx", "kvh"),
        P("ctx", "kvh"),
        P("ctx", "kvh"),
        P("ctx", "kvh"),
        P("ctx"),
        P("ctx"),
        P("ctx"),
        P("kvh", "ctx"),
    )
    return jax.shard_map(
        local, mesh=mesh, in_specs=in_specs, out_specs=P("kvh", "ctx"), check_vma=False
    )
```

time: 646 us -> 67.7 us (0.10)
  the two profiles are of different devices: /device:TPU:1 before, /device:TPU:11 now
where the time goes in v1:
time: 67.7 us; the launch traced here: 67.3 us
  Pallas kernels  59.5 us (88%)
  local copies, waits for them, and re-layouts  7.83 us (12%)
    pallas_call x1, Pallas kernels, local(): pl.pallas_call(kernel, out_shape=jax.ShapeDtypeStruct((4 * ROWS, COLS), B...  59.5 us
    unnamed x19, local copies, waits for them, and re-layouts  7.83 us

profile of v1, /device:TPU:11, one launch (start us, length us, event | category | flops | bytes accessed | tf_op | source)
XLA Modules:
  0.0 67.3 jit_solution(11036248068834531577)
XLA Ops:
  0.0 0.0 copy-start
  0.0 1.0 %copy-done = bf16[2048,128]{1,0:T(8,128)(2,1)S(1)} copy-done((bf16[2048,128]{1,0:T(8,128)(2,1)S(1)}, bf16[2048,128]{1,0:T(8,128)(2,1)}, u32[]{:S(2)}) %copy-start) | copy-done | bytes 524312
  1.0 0.0 copy-start.1
  1.0 1.0 %copy-done.1 = bf16[2048,128]{1,0:T(8,128)(2,1)S(1)} copy-done((bf16[2048,128]{1,0:T(8,128)(2,1)S(1)}, bf16[2048,128]{1,0:T(8,128)(2,1)}, u32[]{:S(2)}) %copy-start.1) | copy-done | bytes 524312
  2.1 0.0 copy-start.2
  2.1 1.0 %copy-done.2 = bf16[1024,256]{1,0:T(8,128)(2,1)S(1)} copy-done((bf16[1024,256]{1,0:T(8,128)(2,1)S(1)}, bf16[1024,256]{1,0:T(8,128)(2,1)}, u32[]{:S(2)}) %copy-start.2) | copy-done | bytes 524312
  3.1 0.0 copy-start.3
  3.1 0.8 %copy-done.3 = bf16[16,1024]{1,0:T(8,128)(2,1)S(1)} copy-done((bf16[16,1024]{1,0:T(8,128)(2,1)S(1)}, bf16[16,1024]{1,0:T(8,128)(2,1)}, u32[]{:S(2)}) %copy-start.3) | copy-done | bytes 32792
  3.9 0.0 copy-start.4
  3.9 0.7 %copy-done.4 = bf16[16,128]{1,0:T(8,128)(2,1)S(1)} copy-done((bf16[16,128]{1,0:T(8,128)(2,1)S(1)}, bf16[16,128]{1,0:T(8,128)(2,1)}, u32[]{:S(2)}) %copy-start.4) | copy-done | bytes 4120
  4.6 0.0 copy-start.5
  4.6 0.7 %copy-done.5 = bf16[16,128]{1,0:T(8,128)(2,1)S(1)} copy-done((bf16[16,128]{1,0:T(8,128)(2,1)S(1)}, bf16[16,128]{1,0:T(8,128)(2,1)}, u32[]{:S(2)}) %copy-start.5) | copy-done | bytes 4120
  5.3 0.0 copy-start.6
  5.3 0.7 copy-done.6
  5.9 0.0 copy-start.7
  5.9 0.7 copy-done.7
  6.6 0.0 copy-start.8
  6.6 0.7 copy-done.8
  7.2 59.5 %shard_map.91 = bf16[64,256]{1,0:T(8,128)(2,1)S(1)} custom-call(bf16[16,1024]{1,0:T(8,128)(2,1)S(1)} %copy-done.3, bf16[2048,128]{1,0:T(8,128)(2,1)S(1)} %copy-done, bf16[2048,128]{1,0:T(8,128)(2,1)S(1)} %copy-done.1, bf16[16,128]{1,0:T(8,128)(2,1)S(1)} %copy-done.4, bf16[16,128]{1,0:T(8,128)(2,1)S(1)} %copy-done.5, s32[16]{0:T(128)S(1)} %copy-done.6, ...), custom_call_target="tpu_custom_call" | custom-call | flops 8999999488 | bytes 2097152 | tf_op jit(solution)/shard_map/pallas_call | solution.py:392
  66.7 0.6 copy.11
Async XLA Ops:
  0.0 1.0 %copy-start = (bf16[2048,128]{1,0:T(8,128)(2,1)S(1)}, bf16[2048,128]{1,0:T(8,128)(2,1)}, u32[]{:S(2)}) copy-start(bf16[2048,128]{1,0:T(8,128)(2,1)} %k_hbm.1) | copy-start | bytes 1572868
  1.0 1.0 %copy-start.1 = (bf16[2048,128]{1,0:T(8,128)(2,1)S(1)}, bf16[2048,128]{1,0:T(8,128)(2,1)}, u32[]{:S(2)}) copy-start(bf16[2048,128]{1,0:T(8,128)(2,1)} %v_hbm.1) | copy-start | bytes 1572868
  2.1 1.0 %copy-start.2 = (bf16[1024,256]{1,0:T(8,128)(2,1)S(1)}, bf16[1024,256]{1,0:T(8,128)(2,1)}, u32[]{:S(2)}) copy-start(bf16[1024,256]{1,0:T(8,128)(2,1)} %w_hbm.1) | copy-start | bytes 1572868
  3.1 0.8 %copy-start.3 = (bf16[16,1024]{1,0:T(8,128)(2,1)S(1)}, bf16[16,1024]{1,0:T(8,128)(2,1)}, u32[]{:S(2)}) copy-start(bf16[16,1024]{1,0:T(8,128)(2,1)} %q_hbm.1) | copy-start | bytes 98308
  3.9 0.7 %copy-start.4 = (bf16[16,128]{1,0:T(8,128)(2,1)S(1)}, bf16[16,128]{1,0:T(8,128)(2,1)}, u32[]{:S(2)}) copy-start(bf16[16,128]{1,0:T(8,128)(2,1)} %ck_hbm.1) | copy-start | bytes 12292
  4.6 0.7 %copy-start.5 = (bf16[16,128]{1,0:T(8,128)(2,1)S(1)}, bf16[16,128]{1,0:T(8,128)(2,1)}, u32[]{:S(2)}) copy-start(bf16[16,128]{1,0:T(8,128)(2,1)} %cv_hbm.1) | copy-start | bytes 12292
  5.3 0.7 copy-start.6
  5.9 0.7 copy-start.7
  6.6 0.7 copy-start.8

commit v2 on v1

v2 whole, which is shorter than its diff:
```python
import math

import jax
import jax.numpy as jnp
from jax import lax
from jax.experimental import pallas as pl
from jax.experimental.pallas import tpu as pltpu
from jax.sharding import PartitionSpec as P

MESH = pl.DeviceIdType.MESH
BF = jnp.bfloat16
F32 = jnp.float32
HEAD = 128
HEADS = 8
ROWS = 16
RINGZ = 8
SHARD = 2048
PAIR = 2 * SHARD
CAND = 2 * ROWS
KPOS = PAIR + CAND
VPOS = PAIR + 128
QH = HEADS * ROWS
QW = HEADS * HEAD + 128
BLK = HEAD + 16
COLS = 256
NEG = -1e30
SCALE = math.log2(math.e) / math.sqrt(HEAD)
CQ = 256
CP = 1024
WROWS = HEADS * HEAD // RINGZ


def split2(x):
    hi = x.astype(BF)
    lo = (x - hi.astype(F32)).astype(BF)
    return hi, lo


def kernel(
    q_hbm, k_hbm, v_hbm, ck_hbm, cv_hbm, len_s, branch_s, depth_s, w_hbm,
    out_ref,
    qall, kbuf, vraw, vt, cvraw, cinfo, wbuf, sa, sb, pbuf, ma, mb, part, got, ysend, yget, blk, attn, prod, terms,
    loc, kv_s, kv_r, w_s, w_r, q_s, q_r, p_s, p_r, y_s, y_r, a_s, a_r, t_s, t_r,
):
    ctx = lax.axis_index("ctx")
    kvh = lax.axis_index("kvh")
    z = ctx // 4
    yh = (ctx // 2) % 2
    core = ctx % 2
    quarter = ctx % 4
    partner = (quarter + 2) % 4

    def plane(dz, so):
        zz = (z + dz) % RINGZ
        yy = (yh + so) % 2
        return (zz * 4 + yy * 2 + core, kvh)

    sibling = (ctx + 1 - 2 * core, kvh)

    def group(j, k):
        return (ctx - quarter + j, k)

    bar = pltpu.get_barrier_semaphore()
    peers = [plane(dz, 0) for dz in range(1, RINGZ)] + [plane(1, 1), plane(RINGZ - 1, 1)]
    peers += [group((quarter + j) % 4, kvh) for j in range(1, 4)]
    peers += [group(j, (kvh + dk) % RINGZ) for dk in range(1, RINGZ) for j in range(4)]
    for peer in peers:
        pl.semaphore_signal(bar, inc=1, device_id=peer, device_id_type=MESH)

    mine = pl.multiple_of(core * SHARD, SHARD)
    cmine = pl.multiple_of(PAIR + core * ROWS, ROWS)
    crow = pl.multiple_of(core * ROWS, ROWS)
    loads = [
        pltpu.make_async_copy(q_hbm, qall.at[0, 0, :, pl.ds(0, HEADS * HEAD)], loc.at[0]),
        pltpu.make_async_copy(k_hbm, kbuf.at[pl.ds(mine, SHARD)], loc.at[1]),
        pltpu.make_async_copy(v_hbm, vraw, loc.at[2]),
        pltpu.make_async_copy(ck_hbm, kbuf.at[pl.ds(cmine, ROWS)], loc.at[3]),
        pltpu.make_async_copy(cv_hbm, cvraw.at[pl.ds(crow, ROWS)], loc.at[4]),
        pltpu.make_async_copy(w_hbm, wbuf.at[quarter], loc.at[5]),
    ]
    for copy in loads:
        copy.start()

    lane = lax.broadcasted_iota(jnp.int32, (ROWS, QH), 1)
    sub = lax.broadcasted_iota(jnp.int32, (ROWS, QH), 0)
    lane_row = lane % ROWS
    meta = jnp.zeros((ROWS, QH), jnp.int32)
    cb = jnp.zeros((ROWS, QH), jnp.int32)
    cd = jnp.zeros((ROWS, QH), jnp.int32)
    for i in range(ROWS):
        n = len_s[i]
        b = branch_s[i]
        d = depth_s[i]
        high = n // 256
        col = jnp.where(
            sub == 0, high, jnp.where(sub == 1, n - high * 256, jnp.where(sub == 2, b, d))
        )
        meta = jnp.where(lane_row == i, col, meta)
        cb = jnp.where(sub == i, b, cb)
        cd = jnp.where(sub == i, d, cd)
    qall[0, 0, :, HEADS * HEAD :] = meta.astype(F32).astype(BF)
    cinfo[core, 0] = cb.astype(F32).astype(BF)
    cinfo[core, 1] = cd.astype(F32).astype(BF)
    pbuf[KPOS:, :] = jnp.zeros((VPOS - KPOS, 2 * QH), BF)
    vt[HEAD:, :] = jnp.ones((BLK - HEAD, VPOS), BF)
    cvraw[CAND:, :] = jnp.zeros((128 - CAND, HEAD), BF)
    for copy in loads:
        copy.wait()
    for j in range(0, SHARD, 128):
        vt[0:HEAD, pl.ds(pl.multiple_of(mine + j, 128), 128)] = vraw[j : j + 128, :].T

    pl.semaphore_wait(bar, len(peers))

    def swap(n, ref):
        return pltpu.make_async_remote_copy(
            src_ref=ref, dst_ref=ref, send_sem=kv_s.at[n], recv_sem=kv_r.at[n],
            device_id=sibling, device_id_type=MESH,
        )

    def swaps(side):
        base = pl.multiple_of(side * SHARD, SHARD)
        cbase = pl.multiple_of(PAIR + side * ROWS, ROWS)
        rbase = pl.multiple_of(side * ROWS, ROWS)
        return [
            swap(0, kbuf.at[pl.ds(base, SHARD)]),
            swap(1, kbuf.at[pl.ds(cbase, ROWS)]),
            swap(2, cvraw.at[pl.ds(rbase, ROWS)]),
            swap(3, cinfo.at[side]),
            swap(4, vt.at[pl.ds(0, HEAD), pl.ds(base, SHARD)]),
            swap(5, wbuf.at[quarter - core + side]),
        ]

    def arrival(dz, so, dst, recv):
        return pltpu.make_async_remote_copy(
            src_ref=dst.at[dz, so], dst_ref=dst.at[dz, so], send_sem=recv.at[dz * 2 + so],
            recv_sem=recv.at[dz * 2 + so], device_id=plane(dz, so), device_id_type=MESH,
        )

    def query_out(dz, so, fwd):
        back = (RINGZ - dz) % RINGZ
        slot = (so + fwd) % 2
        return pltpu.make_async_remote_copy(
            src_ref=qall.at[0, fwd], dst_ref=qall.at[back, slot], send_sem=q_s.at[dz * 3 + so + 2 * fwd],
            recv_sem=q_r.at[back * 2 + slot], device_id=plane(dz, so), device_id_type=MESH,
        )

    direct = [(0, 1), (1, 1), (7, 1), (1, 0), (7, 0), (2, 0), (6, 0), (3, 0), (5, 0), (4, 0)]
    q_out = [query_out(dz, so, 0) for dz, so in direct]
    for copy in q_out:
        copy.start()
    out_swaps = swaps(core)
    in_swaps = swaps(1 - core)
    for copy in out_swaps:
        copy.start()

    def w_across(n, slab):
        rows = pl.ds(n * WROWS, WROWS)
        return pltpu.make_async_remote_copy(
            src_ref=wbuf.at[slab, rows], dst_ref=wbuf.at[slab, rows], send_sem=w_s.at[n],
            recv_sem=w_r.at[n], device_id=plane(0, 1), device_id_type=MESH,
        )

    def w_relay(slab):
        return pltpu.make_async_remote_copy(
            src_ref=wbuf.at[slab], dst_ref=wbuf.at[slab], send_sem=w_s.at[RINGZ],
            recv_sem=w_r.at[RINGZ], device_id=sibling, device_id_type=MESH,
        )

    arrival(0, 1, qall, q_r).wait_recv()
    for dz in (2, 6, 3, 5, 4):
        copy = query_out(dz, 0, 1)
        copy.start()
        q_out.append(copy)
    for n in range(4):
        in_swaps[n].wait_recv()

    base = (ctx - core) * SHARD
    pos_sub = lax.broadcasted_iota(jnp.int32, (CQ, QH), 0)

    def read_stats(st):
        return st[0:1] + st[1:2] + st[2:3], st[3:4] + st[4:5]

    def write_stats(m, total):
        m_hi = m.astype(BF)
        m_mid, m_lo = split2(m - m_hi.astype(F32))
        l_hi, l_lo = split2(total)
        row = lax.broadcasted_iota(jnp.int32, (BLK - HEAD, m.shape[1]), 0)
        stats = jnp.zeros((BLK - HEAD, m.shape[1]), F32)
        for n, x in enumerate((m_hi, m_mid, m_lo, l_hi, l_lo)):
            stats = jnp.where(row == n, x.astype(F32), stats)
        return stats.astype(BF)

    def load_q(dz):
        parts = []
        infos = []
        for so in range(2):
            for h in range(HEADS):
                parts.append(qall[dz, so, :, h * HEAD : (h + 1) * HEAD])
            infos.append(qall[dz, so, :, HEADS * HEAD :].astype(F32))
        q = jnp.concatenate(parts, axis=0).astype(F32) * SCALE
        hi, lo = split2(q)
        lens = [(f[0:1] * 256.0 + f[1:2]).astype(jnp.int32) - base for f in infos]
        return jnp.concatenate([hi, lo], axis=1), lens, infos

    def score(q, pos, width):
        k = kbuf[pos : pos + width, :]
        return lax.dot_general(
            jnp.concatenate([k, k], axis=1), q, (((1,), (1,)), ((), ())),
            preferred_element_type=F32,
        )

    def fused(dz_new, dz_old, parity):
        s_new, s_old = (sa, sb) if parity == 0 else (sb, sa)
        m_new, m_old = (ma, mb) if parity == 0 else (mb, ma)
        if dz_new is not None:
            q, lens, infos = load_q(dz_new)
            top = jnp.full((8, 2 * QH), NEG, F32)
            s = score(q, PAIR, CAND)
            cbr = jnp.concatenate([cinfo[0, 0], cinfo[1, 0]], axis=0).astype(F32)
            cde = jnp.concatenate([cinfo[0, 1], cinfo[1, 1]], axis=0).astype(F32)
            s = jnp.concatenate(
                [
                    jnp.where(
                        (cbr == f[2:3]) & (cde <= f[3:4]), s[:, n * QH : (n + 1) * QH], NEG
                    )
                    for n, f in enumerate(infos)
                ],
                axis=1,
            )
            s_new[PAIR:KPOS, :] = s
            for j in range(0, CAND, 8):
                top = jnp.maximum(top, s[j : j + 8, :])
        if dz_old is not None:
            m = m_old[0:1, :]
            acc = None
            start = 0
        for pos in range(0, PAIR, CQ):
            if dz_new is not None:
                s = score(q, pos, CQ)
                s = jnp.concatenate(
                    [
                        jnp.where(pos_sub < n - pos, s[:, j * QH : (j + 1) * QH], NEG)
                        for j, n in enumerate(lens)
                    ],
                    axis=1,
                )
                s_new[pos : pos + CQ, :] = s
                for j in range(0, CQ, 8):
                    top = jnp.maximum(top, s[j : j + 8, :])
            if dz_old is not None:
                pbuf[pos : pos + CQ, :] = jnp.exp2(s_old[pos : pos + CQ, :] - m).astype(BF)
                end = pos + CQ
                if end == PAIR:
                    pbuf[PAIR:KPOS, :] = jnp.exp2(s_old[PAIR:KPOS, :] - m).astype(BF)
                    end = VPOS
                if end - start >= CP:
                    term = jnp.dot(
                        vt[:, start:end], pbuf[start:end, :], preferred_element_type=F32
                    )
                    acc = term if acc is None else acc + term
                    start = end
        if dz_old is not None:
            total = acc[HEAD : HEAD + 1]
            stats = write_stats(m, total)
            for so in range(2):
                lanes = slice(so * QH, (so + 1) * QH)
                part[dz_old, so, 0:HEAD, :] = acc[0:HEAD, lanes].astype(BF)
                part[dz_old, so, HEAD:, :] = stats[:, lanes]
        if dz_new is not None:
            m_new[...] = jnp.broadcast_to(jnp.max(top, axis=0, keepdims=True), (8, 2 * QH))

    def part_out(dz):
        back = (RINGZ - dz) % RINGZ
        return pltpu.make_async_remote_copy(
            src_ref=part.at[dz], dst_ref=got.at[back], send_sem=p_s.at[dz],
            recv_sem=p_r.at[back], device_id=plane(dz, 0), device_id_type=MESH,
        )

    def arrive_q(dz):
        for so in range(2):
            arrival(dz, so, qall, q_r).wait_recv()

    order = [1, 7, 2, 3, 5, 4, 6, 0]

    def nth(t):
        dz = jnp.int32(order[0])
        for n in range(1, RINGZ):
            dz = jnp.where(t == n, order[n], dz)
        return dz

    arrive_q(order[0])
    fused(order[0], None, 0)
    in_swaps[4].wait_recv()
    vt[0:HEAD, PAIR:] = cvraw[...].T
    w_across(0, quarter).start()
    w_across(1, quarter).start()

    def body(i, carry):
        a, b, c = nth(2 * i), nth(2 * i + 1), nth(2 * i + 2)
        w_across(2 * i + 2, quarter).start()
        w_across(2 * i + 3, quarter).start()
        arrive_q(b)
        fused(b, a, 1)
        part_out(a).start()
        arrive_q(c)
        fused(c, b, 0)
        part_out(b).start()
        return carry

    lax.fori_loop(0, 3, body, 0)
    fused(0, order[6], 1)
    part_out(order[6]).start()
    fused(None, 0, 0)
    for so in range(2):
        got[0, so] = part[0, so]
    for n in range(RINGZ):
        w_across(n, partner).wait_recv()
    w_relay(partner).start()

    for dz in range(1, RINGZ):
        pltpu.make_async_remote_copy(
            src_ref=got.at[dz], dst_ref=got.at[dz], send_sem=p_r.at[dz],
            recv_sem=p_r.at[dz], device_id=plane(dz, 0), device_id_type=MESH,
        ).wait_recv()

    def merged(so):
        stats = [read_stats(got[dz, so, HEAD:, :].astype(F32)) for dz in range(RINGZ)]
        top = stats[0][0]
        for m, _ in stats[1:]:
            top = jnp.maximum(top, m)
        acc = jnp.zeros((HEAD, QH), F32)
        total = jnp.zeros((1, QH), F32)
        for dz, (m, l) in enumerate(stats):
            f = jnp.exp2(m - top)
            total = total + l * f
            acc = acc + got[dz, so, 0:HEAD, :].astype(F32) * f
        return acc, top, total

    acc, top, total = merged(1)
    ysend[0:HEAD, :] = acc.astype(BF)
    ysend[HEAD:, :] = write_stats(top, total)
    y_out = pltpu.make_async_remote_copy(
        src_ref=ysend, dst_ref=yget, send_sem=y_s, recv_sem=y_r,
        device_id=plane(0, 1), device_id_type=MESH,
    )
    y_out.start()
    acc, top, total = merged(0)
    y_out.wait_recv()
    m, l = read_stats(yget[HEAD:, :].astype(F32))
    new = jnp.maximum(top, m)
    f = jnp.exp2(top - new)
    g = jnp.exp2(m - new)
    total = total * f + l * g
    acc = acc * f + yget[0:HEAD, :].astype(F32) * g
    own = (acc / total).T.astype(BF)
    for h in range(HEADS):
        blk[:, h * HEAD : (h + 1) * HEAD] = own[h * ROWS : (h + 1) * ROWS, :]

    def attn_out(dz):
        back = (RINGZ - dz) % RINGZ
        return pltpu.make_async_remote_copy(
            src_ref=blk, dst_ref=attn.at[back], send_sem=a_s.at[dz],
            recv_sem=a_r.at[back], device_id=plane(dz, 0), device_id_type=MESH,
        )

    a_out = [attn_out(dz) for dz in (4, 3, 5, 2, 6, 1, 7)]
    for copy in a_out:
        copy.start()
    attn[0] = blk[...]

    in_swaps[5].wait_recv()
    w_relay((partner + 1 - 2 * core)).wait_recv()
    me = kvh * 4 + quarter

    def term_copy(n, j):
        return pltpu.make_async_remote_copy(
            src_ref=prod.at[j, n], dst_ref=terms.at[me], send_sem=t_s.at[j * RINGZ + n],
            recv_sem=t_r.at[me], device_id=group(j, (z + n) % RINGZ), device_id_type=MESH,
        )

    for dz in range(1, RINGZ):
        pltpu.make_async_remote_copy(
            src_ref=attn.at[dz], dst_ref=attn.at[dz], send_sem=a_r.at[dz],
            recv_sem=a_r.at[dz], device_id=plane(dz, 0), device_id_type=MESH,
        ).wait_recv()
    rows = jnp.concatenate([attn[n] for n in range(RINGZ)], axis=0)
    for j in range(4):
        res = jnp.dot(rows, wbuf[j], preferred_element_type=F32).astype(BF)
        for n in range(RINGZ):
            prod[j, n] = res[n * ROWS : (n + 1) * ROWS, :]
        for n in range(RINGZ):
            here = ((z + n) % RINGZ == kvh) & (quarter == j)

            @pl.when(here)
            def _():
                terms[me] = prod[j, n]

            @pl.when(jnp.logical_not(here))
            def _():
                term_copy(n, j).start()

    for idx in range(4 * RINGZ):

        @pl.when(idx != me)
        def _():
            pltpu.make_async_remote_copy(
                src_ref=terms.at[idx], dst_ref=terms.at[idx], send_sem=t_r.at[idx],
                recv_sem=t_r.at[idx], device_id=sibling, device_id_type=MESH,
            ).wait_recv()

    for j in range(4):
        res = terms[j].astype(F32)
        for k in range(1, RINGZ):
            res = res + terms[k * 4 + j].astype(F32)
        out_ref[j * ROWS : (j + 1) * ROWS, :] = res.astype(BF)

    for copy in q_out + out_swaps + a_out + [y_out, w_relay(partner)]:
        copy.wait_send()
    for n in range(RINGZ):
        w_across(n, quarter).wait_send()
    for dz in range(1, RINGZ):
        part_out(dz).wait_send()
    for j in range(4):
        for n in range(RINGZ):

            @pl.when(jnp.logical_not(((z + n) % RINGZ == kvh) & (quarter == j)))
            def _():
                term_copy(n, j).wait_send()


def local(q, k, v, ck, cv, length, branch, depth, w):
    hbm = pl.BlockSpec(memory_space=pl.ANY)
    smem = pl.BlockSpec(memory_space=pltpu.SMEM)
    dma = pltpu.SemaphoreType.DMA
    return pl.pallas_call(
        kernel,
        out_shape=jax.ShapeDtypeStruct((4 * ROWS, COLS), BF),
        in_specs=[hbm] * 5 + [smem] * 3 + [hbm],
        out_specs=pl.BlockSpec(memory_space=pltpu.VMEM),
        scratch_shapes=[
            pltpu.VMEM((RINGZ, 2, ROWS, QW), BF),
            pltpu.VMEM((KPOS, HEAD), BF),
            pltpu.VMEM((SHARD, HEAD), BF),
            pltpu.VMEM((BLK, VPOS), BF),
            pltpu.VMEM((128, HEAD), BF),
            pltpu.VMEM((2, 2, ROWS, QH), BF),
            pltpu.VMEM((4, HEADS * HEAD, COLS), BF),
            pltpu.VMEM((KPOS, 2 * QH), F32),
            pltpu.VMEM((KPOS, 2 * QH), F32),
            pltpu.VMEM((VPOS, 2 * QH), BF),
            pltpu.VMEM((8, 2 * QH), F32),
            pltpu.VMEM((8, 2 * QH), F32),
            pltpu.VMEM((RINGZ, 2, BLK, QH), BF),
            pltpu.VMEM((RINGZ, 2, BLK, QH), BF),
            pltpu.VMEM((BLK, QH), BF),
            pltpu.VMEM((BLK, QH), BF),
            pltpu.VMEM((ROWS, HEADS * HEAD), BF),
            pltpu.VMEM((RINGZ, ROWS, HEADS * HEAD), BF),
            pltpu.VMEM((4, RINGZ, ROWS, COLS), BF),
            pltpu.VMEM((4 * RINGZ, ROWS, COLS), BF),
            dma((6,)), dma((6,)), dma((6,)), dma((9,)), dma((9,)),
            dma((3 * RINGZ,)), dma((2 * RINGZ,)), dma((RINGZ,)), dma((RINGZ,)),
            dma(()), dma(()), dma((RINGZ,)), dma((RINGZ,)), dma((4 * RINGZ,)), dma((4 * RINGZ,)),
        ],
        compiler_params=pltpu.CompilerParams(
            collective_id=0, has_side_effects=True, vmem_limit_bytes=62 * 2**20
        ),
        cost_estimate=pl.CostEstimate(
            flops=9 * 10**9, bytes_accessed=2 * 2**20, transcendentals=2048 * 4224
        ),
    )(q, k, v, ck, cv, length, branch, depth, w)


def solution(mesh):
    in_specs = (
        P("ctx", "kvh"),
        P("ctx", "kvh"),
        P("ctx", "kvh"),
        P("ctx", "kvh"),
        P("ctx", "kvh"),
        P("ctx"),
        P("ctx"),
        P("ctx"),
        P("kvh", "ctx"),
    )
    return jax.shard_map(
        local, mesh=mesh, in_specs=in_specs, out_specs=P("kvh", "ctx"), check_vma=False
    )
```

time: 67.7 us -> 60.9 us (0.90)
  the two profiles are of different devices: /device:TPU:11 before, /device:TPU:1 now
where the time goes in v2:
time: 60.9 us; the launch traced here: 60.7 us
  Pallas kernels  59.4 us (98%)
  local copies, waits for them, and re-layouts  1.38 us (2%)
    pallas_call x1, Pallas kernels, local(): pl.pallas_call(kernel, out_shape=jax.ShapeDtypeStruct((4 * ROWS, COLS), B...  59.4 us
    unnamed x1, local copies, waits for them, and re-layouts  1.38 us

profile of v2, /device:TPU:1, one launch (start us, length us, event | category | flops | bytes accessed | tf_op | source)
XLA Modules:
  0.0 60.7 jit_solution(12092900777435489816)
XLA Ops:
  0.0 59.4 %shard_map.91 = bf16[64,256]{1,0:T(8,128)(2,1)} custom-call(bf16[16,1024]{1,0:T(8,128)(2,1)} %q_hbm.1, bf16[2048,128]{1,0:T(8,128)(2,1)} %k_hbm.1, bf16[2048,128]{1,0:T(8,128)(2,1)} %v_hbm.1, bf16[16,128]{1,0:T(8,128)(2,1)} %ck_hbm.1, bf16[16,128]{1,0:T(8,128)(2,1)} %cv_hbm.1, s32[16]{0:T(128)} %len_s.1, s32[16]{0:T(128)} %branch_s.1, s32[16]{0:T(128)} %depth_s.1, ...), custom_call_target="tpu_custom_call" | custom-call | flops 8999999488 | bytes 2097152 | tf_op jit(solution)/shard_map/pallas_call | solution.py:435
  59.4 1.4 %copy.11 = bf16[64,256]{1,0:T(8,128)(2,1)} copy(bf16[64,256]{1,0:T(8,128)(2,1)} %shard_map.91) | data formatting | bytes 65536

commit v3 on v2

v3 whole, which is shorter than its diff:
```python
import math

import jax
import jax.numpy as jnp
from jax import lax
from jax.experimental import pallas as pl
from jax.experimental.pallas import tpu as pltpu
from jax.sharding import PartitionSpec as P

MESH = pl.DeviceIdType.MESH
BF = jnp.bfloat16
F32 = jnp.float32
HEAD = 128
HEADS = 8
ROWS = 16
RINGZ = 8
SHARD = 2048
PAIR = 2 * SHARD
CAND = 2 * ROWS
KPOS = PAIR + CAND
VPOS = PAIR + 128
QH = HEADS * ROWS
QW = HEADS * HEAD + 128
BLK = HEAD + 16
COLS = 256
NEG = -1e30
SCALE = math.log2(math.e) / math.sqrt(HEAD)
CQ = 256
CP = 1024
WROWS = HEADS * HEAD // RINGZ
W_EARLY = 2
FAR_FIRST = (4, 3, 5, 2, 6, 1, 7)
STEPS = ((0, 8), (6, 10), (1, 4), (9, 7), (11, 5), (13, 3), (15, 12), (2, 14))
ARRIVE = ((8, 6, 10), (4, 12), (2, 14, 1), (9, 7), (11, 5), (13, 3), (15,), ())
JOIN_EARLY = (4, 3)
JOIN_LATE = (5, 2, 6, 1, 7)


def split2(x):
    hi = x.astype(BF)
    lo = (x - hi.astype(F32)).astype(BF)
    return hi, lo


def kernel(
    q_hbm, k_hbm, v_hbm, ck_hbm, cv_hbm, len_hbm, branch_hbm, depth_hbm, w_hbm,
    out_ref,
    ints, qall, kbuf, vraw, vt, cvraw, cinfo, wbuf, sa, sb, pbuf, ma, mb, part, yget, zsend, got, blk, attn, prod, terms,
    loc, kv_s, kv_r, w_s, w_r, q_s, q_r, r_s, y_s, y_r, p_s, p_r, a_s, a_r, t_s, t_r,
):
    ctx = lax.axis_index("ctx")
    kvh = lax.axis_index("kvh")
    z = ctx // 4
    yh = (ctx // 2) % 2
    core = ctx % 2
    quarter = ctx % 4
    partner = (quarter + 2) % 4

    def plane(dz, so):
        zz = (z + dz) % RINGZ
        yy = (yh + so) % 2
        return (zz * 4 + yy * 2 + core, kvh)

    sibling = (ctx + 1 - 2 * core, kvh)

    def group(j, k):
        return (ctx - quarter + j, k)

    bar = pltpu.get_barrier_semaphore()
    peers = [plane(dz, 0) for dz in range(1, RINGZ)]
    peers += [group((quarter + j) % 4, kvh) for j in range(1, 4)]
    peers += [group(j, (kvh + dk) % RINGZ) for dk in range(1, RINGZ) for j in range(4)]
    for peer in peers:
        pl.semaphore_signal(bar, inc=1, device_id=peer, device_id_type=MESH)

    mine = pl.multiple_of(core * SHARD, SHARD)
    cmine = pl.multiple_of(PAIR + core * ROWS, ROWS)
    crow = pl.multiple_of(core * ROWS, ROWS)
    loads = [
        pltpu.make_async_copy(q_hbm, qall.at[0, :, pl.ds(0, HEADS * HEAD)], loc.at[0]),
        pltpu.make_async_copy(len_hbm, ints.at[0], loc.at[6]),
        pltpu.make_async_copy(branch_hbm, ints.at[1], loc.at[7]),
        pltpu.make_async_copy(depth_hbm, ints.at[2], loc.at[8]),
        pltpu.make_async_copy(k_hbm, kbuf.at[pl.ds(mine, SHARD)], loc.at[1]),
        pltpu.make_async_copy(ck_hbm, kbuf.at[pl.ds(cmine, ROWS)], loc.at[3]),
        pltpu.make_async_copy(cv_hbm, cvraw.at[pl.ds(crow, ROWS)], loc.at[4]),
        pltpu.make_async_copy(v_hbm, vraw, loc.at[2]),
        pltpu.make_async_copy(w_hbm, wbuf.at[quarter], loc.at[5]),
    ]
    for copy in loads:
        copy.start()
    for copy in loads[:4]:
        copy.wait()

    lane = lax.broadcasted_iota(jnp.int32, (ROWS, QH), 1)
    sub = lax.broadcasted_iota(jnp.int32, (ROWS, QH), 0)
    lane_row = lane % ROWS
    meta = jnp.zeros((ROWS, QH), jnp.int32)
    cb = jnp.zeros((ROWS, QH), jnp.int32)
    cd = jnp.zeros((ROWS, QH), jnp.int32)
    for i in range(ROWS):
        n = ints[0, i]
        b = ints[1, i]
        d = ints[2, i]
        high = n // 256
        col = jnp.where(
            sub == 0, high, jnp.where(sub == 1, n - high * 256, jnp.where(sub == 2, b, d))
        )
        meta = jnp.where(lane_row == i, col, meta)
        cb = jnp.where(sub == i, b, cb)
        cd = jnp.where(sub == i, d, cd)
    qall[0, :, HEADS * HEAD :] = meta.astype(F32).astype(BF)
    cinfo[core, 0] = cb.astype(F32).astype(BF)
    cinfo[core, 1] = cd.astype(F32).astype(BF)
    pbuf[KPOS:, :] = jnp.zeros((VPOS - KPOS, 2 * QH), BF)
    vt[HEAD:, :] = jnp.ones((BLK - HEAD, VPOS), BF)
    cvraw[CAND:, :] = jnp.zeros((128 - CAND, HEAD), BF)

    def block_to(src, dst, send, recv, peer):
        return pltpu.make_async_remote_copy(
            src_ref=src, dst_ref=dst, send_sem=send, recv_sem=recv, device_id=peer, device_id_type=MESH
        )

    def arrived(dst, recv):
        block_to(dst, dst, recv, recv, sibling).wait_recv()

    across = plane(0, 1)

    def query_z(dz):
        back = (RINGZ - dz) % RINGZ
        return block_to(
            qall.at[0], qall.at[2 * back], q_s.at[dz], q_r.at[2 * back], plane(dz, 0)
        )

    def query_y(dz):
        return block_to(
            qall.at[2 * dz], qall.at[2 * dz + 1], r_s.at[dz], q_r.at[2 * dz + 1], across
        )

    def part_y(dz):
        return block_to(part.at[2 * dz + 1], yget.at[dz], y_s.at[dz], y_r.at[dz], across)

    def part_z(dz):
        back = (RINGZ - dz) % RINGZ
        return block_to(zsend.at[dz], got.at[back], p_s.at[dz], p_r.at[back], plane(dz, 0))

    def w_across(n, slab):
        rows = pl.ds(n * WROWS, WROWS)
        return block_to(
            wbuf.at[slab, rows], wbuf.at[slab, rows], w_s.at[n], w_r.at[n], across
        )

    def w_relay(slab):
        return block_to(wbuf.at[slab], wbuf.at[slab], w_s.at[RINGZ], w_r.at[RINGZ], sibling)

    def swap(n, ref):
        return block_to(ref, ref, kv_s.at[n], kv_r.at[n], sibling)

    def swaps(side):
        base = pl.multiple_of(side * SHARD, SHARD)
        cbase = pl.multiple_of(PAIR + side * ROWS, ROWS)
        rbase = pl.multiple_of(side * ROWS, ROWS)
        return [
            swap(0, kbuf.at[pl.ds(base, SHARD)]),
            swap(1, kbuf.at[pl.ds(cbase, ROWS)]),
            swap(2, cvraw.at[pl.ds(rbase, ROWS)]),
            swap(3, cinfo.at[side]),
            swap(4, vt.at[pl.ds(0, HEAD), pl.ds(base, SHARD)]),
            swap(5, wbuf.at[quarter - core + side]),
        ]

    pl.semaphore_wait(bar, len(peers))
    query_y(0).start()
    for dz in FAR_FIRST:
        query_z(dz).start()
    out_swaps = swaps(core)
    in_swaps = swaps(1 - core)
    for copy in loads[4:7]:
        copy.wait()
    for copy in out_swaps[:4]:
        copy.start()
    loads[7].wait()
    for j in range(0, SHARD, 128):
        vt[0:HEAD, pl.ds(pl.multiple_of(mine + j, 128), 128)] = vraw[j : j + 128, :].T
    out_swaps[4].start()
    loads[8].wait()
    out_swaps[5].start()
    for n in range(W_EARLY):
        w_across(n, quarter).start()

    base = (ctx - core) * SHARD
    pos_sub = lax.broadcasted_iota(jnp.int32, (CQ, QH), 0)

    def read_stats(st):
        return st[0:1] + st[1:2] + st[2:3], st[3:4] + st[4:5]

    def write_stats(m, total):
        m_hi = m.astype(BF)
        m_mid, m_lo = split2(m - m_hi.astype(F32))
        l_hi, l_lo = split2(total)
        row = lax.broadcasted_iota(jnp.int32, (BLK - HEAD, m.shape[1]), 0)
        stats = jnp.zeros((BLK - HEAD, m.shape[1]), F32)
        for n, x in enumerate((m_hi, m_mid, m_lo, l_hi, l_lo)):
            stats = jnp.where(row == n, x.astype(F32), stats)
        return stats.astype(BF)

    def load_q(pair):
        parts = []
        infos = []
        for slot in pair:
            for h in range(HEADS):
                parts.append(qall[slot, :, h * HEAD : (h + 1) * HEAD])
            infos.append(qall[slot, :, HEADS * HEAD :].astype(F32))
        q = jnp.concatenate(parts, axis=0).astype(F32) * SCALE
        hi, lo = split2(q)
        lens = [(f[0:1] * 256.0 + f[1:2]).astype(jnp.int32) - base for f in infos]
        return jnp.concatenate([hi, lo], axis=1), lens, infos

    def score(q, pos, width):
        k = kbuf[pos : pos + width, :]
        return lax.dot_general(
            jnp.concatenate([k, k], axis=1), q, (((1,), (1,)), ((), ())),
            preferred_element_type=F32,
        )

    def fused(new, old, parity):
        s_new, s_old = (sa, sb) if parity == 0 else (sb, sa)
        m_new, m_old = (ma, mb) if parity == 0 else (mb, ma)
        if new is not None:
            q, lens, infos = load_q(new)
            top = jnp.full((8, 2 * QH), NEG, F32)
            s = score(q, PAIR, CAND)
            cbr = jnp.concatenate([cinfo[0, 0], cinfo[1, 0]], axis=0).astype(F32)
            cde = jnp.concatenate([cinfo[0, 1], cinfo[1, 1]], axis=0).astype(F32)
            s = jnp.concatenate(
                [
                    jnp.where(
                        (cbr == f[2:3]) & (cde <= f[3:4]), s[:, n * QH : (n + 1) * QH], NEG
                    )
                    for n, f in enumerate(infos)
                ],
                axis=1,
            )
            s_new[PAIR:KPOS, :] = s
            for j in range(0, CAND, 8):
                top = jnp.maximum(top, s[j : j + 8, :])
        if old is not None:
            m = m_old[0:1, :]
            acc = None
            start = 0
        for pos in range(0, PAIR, CQ):
            if new is not None:
                s = score(q, pos, CQ)
                s = jnp.concatenate(
                    [
                        jnp.where(pos_sub < n - pos, s[:, j * QH : (j + 1) * QH], NEG)
                        for j, n in enumerate(lens)
                    ],
                    axis=1,
                )
                s_new[pos : pos + CQ, :] = s
                for j in range(0, CQ, 8):
                    top = jnp.maximum(top, s[j : j + 8, :])
            if old is not None:
                pbuf[pos : pos + CQ, :] = jnp.exp2(s_old[pos : pos + CQ, :] - m).astype(BF)
                end = pos + CQ
                if end == PAIR:
                    pbuf[PAIR:KPOS, :] = jnp.exp2(s_old[PAIR:KPOS, :] - m).astype(BF)
                    end = VPOS
                if end - start >= CP:
                    term = jnp.dot(
                        vt[:, start:end], pbuf[start:end, :], preferred_element_type=F32
                    )
                    acc = term if acc is None else acc + term
                    start = end
        if old is not None:
            total = acc[HEAD : HEAD + 1]
            stats = write_stats(m, total)
            for n, slot in enumerate(old):
                lanes = slice(n * QH, (n + 1) * QH)
                part[slot, 0:HEAD, :] = acc[0:HEAD, lanes].astype(BF)
                part[slot, HEAD:, :] = stats[:, lanes]
        if new is not None:
            m_new[...] = jnp.broadcast_to(jnp.max(top, axis=0, keepdims=True), (8, 2 * QH))

    def nth(t):
        pair = []
        for side in range(2):
            slot = jnp.int32(STEPS[0][side])
            for n in range(1, RINGZ):
                slot = jnp.where(t == n, STEPS[n][side], slot)
            pair.append(slot)
        return pair

    def ready(t):
        for slot in ARRIVE[t]:
            arrived(qall.at[slot], q_r.at[slot])
            if slot % 2 == 0:
                query_y(slot // 2).start()

    def finished(t):
        for slot in STEPS[t]:
            if slot % 2:
                part_y(slot // 2).start()

    def at(i, fn, steps):
        for n, t in enumerate(steps):
            pl.when(i == n)(lambda t=t: fn(t))

    for n in range(4):
        in_swaps[n].wait_recv()
    ready(0)
    fused(STEPS[0], None, 0)
    in_swaps[4].wait_recv()
    vt[0:HEAD, PAIR:] = cvraw[...].T

    def body(i, carry):
        a, b, c = nth(2 * i), nth(2 * i + 1), nth(2 * i + 2)
        at(i, ready, (1, 3, 5))
        fused(b, a, 1)
        at(i, finished, (0, 2, 4))
        at(i, ready, (2, 4, 6))
        fused(c, b, 0)
        at(i, finished, (1, 3, 5))
        return carry

    lax.fori_loop(0, 3, body, 0)
    ready(7)
    fused(STEPS[7], STEPS[6], 1)
    finished(6)
    for n in range(W_EARLY, RINGZ):
        w_across(n, quarter).start()

    def merge(stats, accs):
        top = stats[0][0]
        for m, _ in stats[1:]:
            top = jnp.maximum(top, m)
        acc = total = None
        for (m, l), x in zip(stats, accs):
            f = jnp.exp2(m - top)
            total = l * f if total is None else total + l * f
            term = x.astype(F32) * f
            acc = term if acc is None else acc + term
        return acc, top, total

    def join(dz, dst):
        arrived(yget.at[dz], y_r.at[dz])
        refs = (part.at[2 * dz], yget.at[dz])
        acc, top, total = merge(
            [read_stats(ref[HEAD:, :].astype(F32)) for ref in refs], [ref[0:HEAD, :] for ref in refs]
        )
        dst[0:HEAD, :] = acc.astype(BF)
        dst[HEAD:, :] = write_stats(top, total)

    for dz in JOIN_EARLY:
        join(dz, zsend.at[dz])
        part_z(dz).start()
    fused(None, STEPS[7], 0)
    for dz in JOIN_LATE:
        join(dz, zsend.at[dz])
        part_z(dz).start()
    join(0, got.at[0])

    for dz in range(1, RINGZ):
        arrived(got.at[dz], p_r.at[dz])
    acc, top, total = merge(
        [read_stats(got[dz, HEAD:, :].astype(F32)) for dz in range(RINGZ)],
        [got[dz, 0:HEAD, :] for dz in range(RINGZ)],
    )
    own = (acc / total).T.astype(BF)
    for h in range(HEADS):
        blk[:, h * HEAD : (h + 1) * HEAD] = own[h * ROWS : (h + 1) * ROWS, :]

    def attn_out(dz):
        back = (RINGZ - dz) % RINGZ
        return block_to(blk, attn.at[back], a_s.at[dz], a_r.at[back], plane(dz, 0))

    for dz in FAR_FIRST:
        attn_out(dz).start()
    attn[0] = blk[...]
    for n in range(RINGZ):
        w_across(n, partner).wait_recv()
    w_relay(partner).start()

    in_swaps[5].wait_recv()
    w_relay((partner + 1 - 2 * core)).wait_recv()
    me = kvh * 4 + quarter

    def term_copy(n, j):
        return block_to(
            prod.at[j, n], terms.at[me], t_s.at[j * RINGZ + n], t_r.at[me],
            group(j, (z + n) % RINGZ),
        )

    for dz in range(1, RINGZ):
        arrived(attn.at[dz], a_r.at[dz])
    rows = jnp.concatenate([attn[n] for n in range(RINGZ)], axis=0)
    for j in range(4):
        res = jnp.dot(rows, wbuf[j], preferred_element_type=F32).astype(BF)
        for n in range(RINGZ):
            prod[j, n] = res[n * ROWS : (n + 1) * ROWS, :]
        for n in range(RINGZ):
            here = ((z + n) % RINGZ == kvh) & (quarter == j)

            @pl.when(here)
            def _():
                terms[me] = prod[j, n]

            @pl.when(jnp.logical_not(here))
            def _():
                term_copy(n, j).start()

    for idx in range(4 * RINGZ):

        @pl.when(idx != me)
        def _():
            arrived(terms.at[idx], t_r.at[idx])

    for j in range(4):
        res = terms[j].astype(F32)
        for k in range(1, RINGZ):
            res = res + terms[k * 4 + j].astype(F32)
        out_ref[j * ROWS : (j + 1) * ROWS, :] = res.astype(BF)

    for copy in out_swaps + [w_relay(partner)]:
        copy.wait_send()
    for dz in range(RINGZ):
        query_y(dz).wait_send()
        part_y(dz).wait_send()
        w_across(dz, quarter).wait_send()
        if dz:
            query_z(dz).wait_send()
            part_z(dz).wait_send()
            attn_out(dz).wait_send()
    for j in range(4):
        for n in range(RINGZ):

            @pl.when(jnp.logical_not(((z + n) % RINGZ == kvh) & (quarter == j)))
            def _():
                term_copy(n, j).wait_send()


def local(q, k, v, ck, cv, length, branch, depth, w):
    hbm = pl.BlockSpec(memory_space=pl.ANY)
    dma = pltpu.SemaphoreType.DMA
    return pl.pallas_call(
        kernel,
        out_shape=jax.ShapeDtypeStruct((4 * ROWS, COLS), BF),
        in_specs=[hbm] * 9,
        out_specs=pl.BlockSpec(memory_space=pltpu.VMEM),
        scratch_shapes=[
            pltpu.SMEM((3, ROWS), jnp.int32),
            pltpu.VMEM((2 * RINGZ, ROWS, QW), BF),
            pltpu.VMEM((KPOS, HEAD), BF),
            pltpu.VMEM((SHARD, HEAD), BF),
            pltpu.VMEM((BLK, VPOS), BF),
            pltpu.VMEM((128, HEAD), BF),
            pltpu.VMEM((2, 2, ROWS, QH), BF),
            pltpu.VMEM((4, HEADS * HEAD, COLS), BF),
            pltpu.VMEM((KPOS, 2 * QH), F32),
            pltpu.VMEM((KPOS, 2 * QH), F32),
            pltpu.VMEM((VPOS, 2 * QH), BF),
            pltpu.VMEM((8, 2 * QH), F32),
            pltpu.VMEM((8, 2 * QH), F32),
            pltpu.VMEM((2 * RINGZ, BLK, QH), BF),
            pltpu.VMEM((RINGZ, BLK, QH), BF),
            pltpu.VMEM((RINGZ, BLK, QH), BF),
            pltpu.VMEM((RINGZ, BLK, QH), BF),
            pltpu.VMEM((ROWS, HEADS * HEAD), BF),
            pltpu.VMEM((RINGZ, ROWS, HEADS * HEAD), BF),
            pltpu.VMEM((4, RINGZ, ROWS, COLS), BF),
            pltpu.VMEM((4 * RINGZ, ROWS, COLS), BF),
            dma((9,)), dma((6,)), dma((6,)), dma((9,)), dma((9,)),
            dma((RINGZ,)), dma((2 * RINGZ,)), dma((RINGZ,)),
            dma((RINGZ,)), dma((RINGZ,)), dma((RINGZ,)), dma((RINGZ,)),
            dma((RINGZ,)), dma((RINGZ,)), dma((4 * RINGZ,)), dma((4 * RINGZ,)),
        ],
        compiler_params=pltpu.CompilerParams(
            collective_id=0, has_side_effects=True, vmem_limit_bytes=62 * 2**20
        ),
        cost_estimate=pl.CostEstimate(
            flops=9 * 10**9, bytes_accessed=2 * 2**20, transcendentals=2048 * 4224
        ),
    )(q, k, v, ck, cv, length, branch, depth, w)


def solution(mesh):
    in_specs = (
        P("ctx", "kvh"),
        P("ctx", "kvh"),
        P("ctx", "kvh"),
        P("ctx", "kvh"),
        P("ctx", "kvh"),
        P("ctx"),
        P("ctx"),
        P("ctx"),
        P("kvh", "ctx"),
    )
    return jax.shard_map(
        local, mesh=mesh, in_specs=in_specs, out_specs=P("kvh", "ctx"), check_vma=False
    )
```

time: 60.9 us -> 53.9 us (0.89)
  Pallas kernels: 59.4 us -> 52.3 us
    pallas_call x1, Pallas kernels: 59.4 us -> 52.3 us  [local(): pl.pallas_call(kernel, out_shape=jax.ShapeDtypeStruct((4 * ROWS, COLS), B...]
where the time goes in v3:
time: 53.9 us; the launch traced here: 53.7 us
  Pallas kernels  52.3 us (97%)
  local copies, waits for them, and re-layouts  1.38 us (3%)
    pallas_call x1, Pallas kernels, local(): pl.pallas_call(kernel, out_shape=jax.ShapeDtypeStruct((4 * ROWS, COLS), B...  52.3 us
    unnamed x1, local copies, waits for them, and re-layouts  1.38 us

profile of v3, /device:TPU:1, one launch (start us, length us, event | category | flops | bytes accessed | tf_op | source)
XLA Modules:
  0.0 53.7 jit_solution(8756306481774527358)
XLA Ops:
  0.0 52.3 %shard_map.91 = bf16[64,256]{1,0:T(8,128)(2,1)} custom-call(bf16[16,1024]{1,0:T(8,128)(2,1)} %q_hbm.1, bf16[2048,128]{1,0:T(8,128)(2,1)} %k_hbm.1, bf16[2048,128]{1,0:T(8,128)(2,1)} %v_hbm.1, bf16[16,128]{1,0:T(8,128)(2,1)} %ck_hbm.1, bf16[16,128]{1,0:T(8,128)(2,1)} %cv_hbm.1, s32[16]{0:T(128)} %len_hbm.1, s32[16]{0:T(128)} %branch_hbm.1, s32[16]{0:T(128)} %depth_hbm.1, ...), custom_call_target="tpu_custom_call" | custom-call | flops 8999999488 | bytes 2097152 | tf_op jit(solution)/shard_map/pallas_call | solution.py:446
  52.4 1.4 %copy.11 = bf16[64,256]{1,0:T(8,128)(2,1)} copy(bf16[64,256]{1,0:T(8,128)(2,1)} %shard_map.91) | data formatting | bytes 65536

commit v4 on v3

--- a/solution.py
+++ b/solution.py
@@ -28,12 +28,13 @@
 CQ = 256
 CP = 1024
 WROWS = HEADS * HEAD // RINGZ
-W_EARLY = 2
 FAR_FIRST = (4, 3, 5, 2, 6, 1, 7)
-STEPS = ((0, 8), (6, 10), (1, 4), (9, 7), (11, 5), (13, 3), (15, 12), (2, 14))
-ARRIVE = ((8, 6, 10), (4, 12), (2, 14, 1), (9, 7), (11, 5), (13, 3), (15,), ())
-JOIN_EARLY = (4, 3)
-JOIN_LATE = (5, 2, 6, 1, 7)
+QUERY_ORDER = ((1, 0), (7, 0), (0, 1), (2, 0), (6, 0), (3, 0), (5, 0), (4, 0))
+JOINED = ()
+JOIN_EARLY = 0
+STEPS = ((0, 2), (14, 4), (1, 12), (6, 10), (3, 15), (5, 13), (7, 11), (9, 8))
+ARRIVE = ((2, 14), (4, 12), (1, 6, 10), (8,), (3, 15), (5, 13), (7, 11), (9,))
+W_AT = (0, 0, 0, 1, 2, 3, 4, 5, 8)
 
 
 def split2(x):
@@ -44,9 +45,9 @@
 
 def kernel(
     q_hbm, k_hbm, v_hbm, ck_hbm, cv_hbm, len_hbm, branch_hbm, depth_hbm, w_hbm,
-    out_ref,
-    ints, qall, kbuf, vraw, vt, cvraw, cinfo, wbuf, sa, sb, pbuf, ma, mb, part, yget, zsend, got, blk, attn, prod, terms,
-    loc, kv_s, kv_r, w_s, w_r, q_s, q_r, r_s, y_s, y_r, p_s, p_r, a_s, a_r, t_s, t_r,
+    terms,
+    ints, qall, kbuf, vraw, vt, cvraw, cinfo, wbuf, sa, sb, pbuf, ma, mb, part, yget, zsend, got, gotd, blk, attn, prod,
+    loc, kv_s, kv_r, w_s, w_r, q_s, q_r, r_s, y_s, y_r, p_s, p_r, d_r, a_s, a_r, t_s, t_r,
 ):
     ctx = lax.axis_index("ctx")
     kvh = lax.axis_index("kvh")
@@ -67,7 +68,7 @@
         return (ctx - quarter + j, k)
 
     bar = pltpu.get_barrier_semaphore()
-    peers = [plane(dz, 0) for dz in range(1, RINGZ)]
+    peers = [plane(dz, so) for dz in range(1, RINGZ) for so in range(2)]
     peers += [group((quarter + j) % 4, kvh) for j in range(1, 4)]
     peers += [group(j, (kvh + dk) % RINGZ) for dk in range(1, RINGZ) for j in range(4)]
     for peer in peers:
@@ -132,6 +133,12 @@
             qall.at[0], qall.at[2 * back], q_s.at[dz], q_r.at[2 * back], plane(dz, 0)
         )
 
+    def query_d(dz):
+        back = (RINGZ - dz) % RINGZ
+        return block_to(
+            qall.at[0], qall.at[2 * back + 1], r_s.at[dz], q_r.at[2 * back + 1], plane(dz, 1)
+        )
+
     def query_y(dz):
         return block_to(
             qall.at[2 * dz], qall.at[2 * dz + 1], r_s.at[dz], q_r.at[2 * dz + 1], across
@@ -142,7 +149,14 @@
 
     def part_z(dz):
         back = (RINGZ - dz) % RINGZ
-        return block_to(zsend.at[dz], got.at[back], p_s.at[dz], p_r.at[back], plane(dz, 0))
+        src = zsend.at[dz] if dz in JOINED else part.at[2 * dz]
+        return block_to(src, got.at[back], p_s.at[dz], p_r.at[back], plane(dz, 0))
+
+    def part_d(dz):
+        back = (RINGZ - dz) % RINGZ
+        return block_to(
+            part.at[2 * dz + 1], gotd.at[back], y_s.at[dz], d_r.at[back], plane(dz, 1)
+        )
 
     def w_across(n, slab):
         rows = pl.ds(n * WROWS, WROWS)
@@ -170,9 +184,8 @@
         ]
 
     pl.semaphore_wait(bar, len(peers))
-    query_y(0).start()
-    for dz in FAR_FIRST:
-        query_z(dz).start()
+    for dz, so in QUERY_ORDER:
+        (query_d(dz) if dz and so else query_y(0) if so else query_z(dz)).start()
     out_swaps = swaps(core)
     in_swaps = swaps(1 - core)
     for copy in loads[4:7]:
@@ -185,9 +198,6 @@
     out_swaps[4].start()
     loads[8].wait()
     out_swaps[5].start()
-    for n in range(W_EARLY):
-        w_across(n, quarter).start()
-
     base = (ctx - core) * SHARD
     pos_sub = lax.broadcasted_iota(jnp.int32, (CQ, QH), 0)
 
@@ -295,13 +305,18 @@
     def ready(t):
         for slot in ARRIVE[t]:
             arrived(qall.at[slot], q_r.at[slot])
-            if slot % 2 == 0:
+            if slot % 2 == 0 and (slot // 2, 1) not in QUERY_ORDER:
                 query_y(slot // 2).start()
 
     def finished(t):
         for slot in STEPS[t]:
+            dz = slot // 2
             if slot % 2:
-                part_y(slot // 2).start()
+                (part_y if dz in JOINED or dz == 0 else part_d)(dz).start()
+            elif dz and dz not in JOINED:
+                part_z(dz).start()
+        for n in range(W_AT[t], W_AT[t + 1]):
+            w_across(n, quarter).start()
 
     def at(i, fn, steps):
         for n, t in enumerate(steps):
@@ -328,9 +343,6 @@
     ready(7)
     fused(STEPS[7], STEPS[6], 1)
     finished(6)
-    for n in range(W_EARLY, RINGZ):
-        w_across(n, quarter).start()
-
     def merge(stats, accs):
         top = stats[0][0]
         for m, _ in stats[1:]:
@@ -352,20 +364,25 @@
         dst[0:HEAD, :] = acc.astype(BF)
         dst[HEAD:, :] = write_stats(top, total)
 
-    for dz in JOIN_EARLY:
+    for dz in JOINED[:JOIN_EARLY]:
         join(dz, zsend.at[dz])
         part_z(dz).start()
     fused(None, STEPS[7], 0)
-    for dz in JOIN_LATE:
+    finished(7)
+    for dz in JOINED[JOIN_EARLY:]:
         join(dz, zsend.at[dz])
         part_z(dz).start()
     join(0, got.at[0])
 
     for dz in range(1, RINGZ):
         arrived(got.at[dz], p_r.at[dz])
+    singles = [dz for dz in range(1, RINGZ) if dz not in JOINED]
+    for dz in singles:
+        back = RINGZ - dz
+        arrived(gotd.at[back], d_r.at[back])
+    refs = [got.at[dz] for dz in range(RINGZ)] + [gotd.at[(RINGZ - dz) % RINGZ] for dz in singles]
     acc, top, total = merge(
-        [read_stats(got[dz, HEAD:, :].astype(F32)) for dz in range(RINGZ)],
-        [got[dz, 0:HEAD, :] for dz in range(RINGZ)],
+        [read_stats(ref[HEAD:, :].astype(F32)) for ref in refs], [ref[0:HEAD, :] for ref in refs]
     )
     own = (acc / total).T.astype(BF)
     for h in range(HEADS):
@@ -386,68 +403,77 @@
     w_relay((partner + 1 - 2 * core)).wait_recv()
     me = kvh * 4 + quarter
 
-    def term_copy(n, j):
+    def term_copy(i, n):
         return block_to(
-            prod.at[j, n], terms.at[me], t_s.at[j * RINGZ + n], t_r.at[me],
-            group(j, (z + n) % RINGZ),
-        )
+            prod.at[i, n], terms.at[me], t_s.at[i * RINGZ + n], t_r.at[me],
+            group((quarter + i) % 4, (z + n) % RINGZ),
+        )
+
+    def own_term(n):
+        return pltpu.make_async_copy(prod.at[0, n], terms.at[me], t_s.at[n])
 
     for dz in range(1, RINGZ):
         arrived(attn.at[dz], a_r.at[dz])
     rows = jnp.concatenate([attn[n] for n in range(RINGZ)], axis=0)
-    for j in range(4):
+    for i in (2, 3, 1, 0):
+        j = (quarter + i) % 4
         res = jnp.dot(rows, wbuf[j], preferred_element_type=F32).astype(BF)
         for n in range(RINGZ):
-            prod[j, n] = res[n * ROWS : (n + 1) * ROWS, :]
+            prod[i, n] = res[n * ROWS : (n + 1) * ROWS, :]
         for n in range(RINGZ):
-            here = ((z + n) % RINGZ == kvh) & (quarter == j)
-
-            @pl.when(here)
-            def _():
-                terms[me] = prod[j, n]
-
-            @pl.when(jnp.logical_not(here))
-            def _():
-                term_copy(n, j).start()
-
-    for idx in range(4 * RINGZ):
-
-        @pl.when(idx != me)
-        def _():
-            arrived(terms.at[idx], t_r.at[idx])
-
-    for j in range(4):
-        res = terms[j].astype(F32)
-        for k in range(1, RINGZ):
-            res = res + terms[k * 4 + j].astype(F32)
-        out_ref[j * ROWS : (j + 1) * ROWS, :] = res.astype(BF)
+            if i:
+                term_copy(i, n).start()
+            else:
+                here = (z + n) % RINGZ == kvh
+
+                @pl.when(here)
+                def _():
+                    own_term(n).start()
+
+                @pl.when(jnp.logical_not(here))
+                def _():
+                    term_copy(i, n).start()
 
     for copy in out_swaps + [w_relay(partner)]:
         copy.wait_send()
     for dz in range(RINGZ):
-        query_y(dz).wait_send()
-        part_y(dz).wait_send()
+        (query_d if dz and (dz, 1) in QUERY_ORDER else query_y)(dz).wait_send()
+        (part_y if dz in JOINED or dz == 0 else part_d)(dz).wait_send()
         w_across(dz, quarter).wait_send()
         if dz:
             query_z(dz).wait_send()
             part_z(dz).wait_send()
             attn_out(dz).wait_send()
-    for j in range(4):
+    for i in range(4):
         for n in range(RINGZ):
-
-            @pl.when(jnp.logical_not(((z + n) % RINGZ == kvh) & (quarter == j)))
-            def _():
-                term_copy(n, j).wait_send()
+            if i:
+                term_copy(i, n).wait_send()
+            else:
+                here = (z + n) % RINGZ == kvh
+
+                @pl.when(here)
+                def _():
+                    own_term(n).wait()
+
+                @pl.when(jnp.logical_not(here))
+                def _():
+                    term_copy(i, n).wait_send()
+
+    for idx in range(4 * RINGZ):
+
+        @pl.when(idx != me)
+        def _():
+            arrived(terms.at[idx], t_r.at[idx])
 
 
 def local(q, k, v, ck, cv, length, branch, depth, w):
     hbm = pl.BlockSpec(memory_space=pl.ANY)
     dma = pltpu.SemaphoreType.DMA
-    return pl.pallas_call(
+    terms = pl.pallas_call(
         kernel,
-        out_shape=jax.ShapeDtypeStruct((4 * ROWS, COLS), BF),
+        out_shape=jax.ShapeDtypeStruct((4 * RINGZ, ROWS, COLS), BF),
         in_specs=[hbm] * 9,
-        out_specs=pl.BlockSpec(memory_space=pltpu.VMEM),
+        out_specs=hbm,
         scratch_shapes=[
             pltpu.SMEM((3, ROWS), jnp.int32),
             pltpu.VMEM((2 * RINGZ, ROWS, QW), BF),
@@ -466,13 +492,13 @@
             pltpu.VMEM((RINGZ, BLK, QH), BF),
             pltpu.VMEM((RINGZ, BLK, QH), BF),
             pltpu.VMEM((RINGZ, BLK, QH), BF),
+            pltpu.VMEM((RINGZ, BLK, QH), BF),
             pltpu.VMEM((ROWS, HEADS * HEAD), BF),
             pltpu.VMEM((RINGZ, ROWS, HEADS * HEAD), BF),
             pltpu.VMEM((4, RINGZ, ROWS, COLS), BF),
-            pltpu.VMEM((4 * RINGZ, ROWS, COLS), BF),
             dma((9,)), dma((6,)), dma((6,)), dma((9,)), dma((9,)),
             dma((RINGZ,)), dma((2 * RINGZ,)), dma((RINGZ,)),
-            dma((RINGZ,)), dma((RINGZ,)), dma((RINGZ,)), dma((RINGZ,)),
+            dma((RINGZ,)), dma((RINGZ,)), dma((RINGZ,)), dma((RINGZ,)), dma((RINGZ,)),
             dma((RINGZ,)), dma((RINGZ,)), dma((4 * RINGZ,)), dma((4 * RINGZ,)),
         ],
         compiler_params=pltpu.CompilerParams(
@@ -482,6 +508,8 @@
             flops=9 * 10**9, bytes_accessed=2 * 2**20, transcendentals=2048 * 4224
         ),
     )(q, k, v, ck, cv, length, branch, depth, w)
+    terms = terms.reshape(RINGZ, 4 * ROWS, COLS).astype(F32)
+    return jnp.sum(terms, axis=0).astype(BF)
 
 
 def solution(mesh):

time: 53.9 us -> 53.7 us (level)
  other arithmetic: 0 us -> 1.61 us
  local copies, waits for them, and re-layouts: 1.38 us -> 0 us
    reduce_sum x0 -> x1, other arithmetic: none -> 1.61 us  [local(): return jnp.sum(terms, axis=0).astype(BF)]
    unnamed x1 -> x0, local copies, waits for them, and re-layouts: 1.38 us -> none
where the time goes in v4:
time: 53.7 us; the launch traced here: 53.6 us
  Pallas kernels  52 us (97%)
  other arithmetic  1.61 us (3%)
    pallas_call x1, Pallas kernels, local(): pl.pallas_call(kernel, out_shape=jax.ShapeDtypeStruct((4 * RINGZ, ROWS, C...  52 us
    reduce_sum x1, other arithmetic, local(): return jnp.sum(terms, axis=0).astype(BF)  1.61 us

profile of v4, /device:TPU:1, one launch (start us, length us, event | category | flops | bytes accessed | tf_op | source)
XLA Modules:
  0.0 53.6 jit_solution(3073139093678326161)
XLA Ops:
  0.0 52.0 %shard_map.91 = bf16[32,16,256]{2,1,0:T(8,128)(2,1)} custom-call(bf16[16,1024]{1,0:T(8,128)(2,1)} %q_hbm.1, bf16[2048,128]{1,0:T(8,128)(2,1)} %k_hbm.1, bf16[2048,128]{1,0:T(8,128)(2,1)} %v_hbm.1, bf16[16,128]{1,0:T(8,128)(2,1)} %ck_hbm.1, bf16[16,128]{1,0:T(8,128)(2,1)} %cv_hbm.1, s32[16]{0:T(128)} %len_hbm.1, s32[16]{0:T(128)} %branch_hbm.1, s32[16]{0:T(128)} %depth_hbm.1, ...), custom_call_target="tpu_custom_call" | custom-call | flops 8999999488 | bytes 2097152 | tf_op jit(solution)/shard_map/pallas_call | solution.py:472
  52.0 1.6 %bitcast_reduce_fusion = bf16[64,256]{1,0:T(8,128)(2,1)} fusion(bf16[8,64,256]{2,1,0:T(8,128)(2,1)} %bitcast.3), kind=kLoop, calls=%fused_computation | loop fusion | flops 114688 | bytes 294912 | tf_op jit(solution)/shard_map/reduce_sum | solution.py:512

commit v5 on v4

--- a/solution.py
+++ b/solution.py
@@ -29,11 +29,11 @@
 CP = 1024
 WROWS = HEADS * HEAD // RINGZ
 FAR_FIRST = (4, 3, 5, 2, 6, 1, 7)
-QUERY_ORDER = ((1, 0), (7, 0), (0, 1), (2, 0), (6, 0), (3, 0), (5, 0), (4, 0))
+QUERY_ORDER = ((1, 0), (7, 0), (0, 1), (2, 0), (6, 0), (4, 0), (3, 0), (5, 0))
 JOINED = ()
 JOIN_EARLY = 0
-STEPS = ((0, 2), (14, 4), (1, 12), (6, 10), (3, 15), (5, 13), (7, 11), (9, 8))
-ARRIVE = ((2, 14), (4, 12), (1, 6, 10), (8,), (3, 15), (5, 13), (7, 11), (9,))
+STEPS = ((0, 2), (14, 4), (1, 12), (6, 10), (3, 15), (5, 13), (9, 7), (11, 8))
+ARRIVE = ((2, 14), (4, 12), (1, 8), (6, 10), (3, 15), (5, 13), (9, 7), (11,))
 W_AT = (0, 0, 0, 1, 2, 3, 4, 5, 8)
 
 

time: 53.7 us -> 53.3 us (level)
  no operation moved by 1% of the time
where the time goes in v5:
time: 53.3 us; the launch traced here: 53.2 us
  Pallas kernels  51.5 us (97%)
  other arithmetic  1.61 us (3%)
    pallas_call x1, Pallas kernels, local(): pl.pallas_call(kernel, out_shape=jax.ShapeDtypeStruct((4 * RINGZ, ROWS, C...  51.5 us
    reduce_sum x1, other arithmetic, local(): return jnp.sum(terms, axis=0).astype(BF)  1.61 us

profile of v5, /device:TPU:1, one launch (start us, length us, event | category | flops | bytes accessed | tf_op | source)
XLA Modules:
  0.0 53.2 jit_solution(6453260437359005295)
XLA Ops:
  0.0 51.5 %shard_map.91 = bf16[32,16,256]{2,1,0:T(8,128)(2,1)} custom-call(bf16[16,1024]{1,0:T(8,128)(2,1)} %q_hbm.1, bf16[2048,128]{1,0:T(8,128)(2,1)} %k_hbm.1, bf16[2048,128]{1,0:T(8,128)(2,1)} %v_hbm.1, bf16[16,128]{1,0:T(8,128)(2,1)} %ck_hbm.1, bf16[16,128]{1,0:T(8,128)(2,1)} %cv_hbm.1, s32[16]{0:T(128)} %len_hbm.1, s32[16]{0:T(128)} %branch_hbm.1, s32[16]{0:T(128)} %depth_hbm.1, ...), custom_call_target="tpu_custom_call" | custom-call | flops 8999999488 | bytes 2097152 | tf_op jit(solution)/shard_map/pallas_call | solution.py:472
  51.6 1.6 %bitcast_reduce_fusion = bf16[64,256]{1,0:T(8,128)(2,1)} fusion(bf16[8,64,256]{2,1,0:T(8,128)(2,1)} %bitcast.3), kind=kLoop, calls=%fused_computation | loop fusion | flops 114688 | bytes 294912 | tf_op jit(solution)/shard_map/reduce_sum | solution.py:512

commit v6 on v5

--- a/solution.py
+++ b/solution.py
@@ -412,27 +412,29 @@
     def own_term(n):
         return pltpu.make_async_copy(prod.at[0, n], terms.at[me], t_s.at[n])
 
-    for dz in range(1, RINGZ):
-        arrived(attn.at[dz], a_r.at[dz])
-    rows = jnp.concatenate([attn[n] for n in range(RINGZ)], axis=0)
-    for i in (2, 3, 1, 0):
-        j = (quarter + i) % 4
-        res = jnp.dot(rows, wbuf[j], preferred_element_type=F32).astype(BF)
-        for n in range(RINGZ):
-            prod[i, n] = res[n * ROWS : (n + 1) * ROWS, :]
-        for n in range(RINGZ):
-            if i:
-                term_copy(i, n).start()
-            else:
-                here = (z + n) % RINGZ == kvh
-
-                @pl.when(here)
-                def _():
-                    own_term(n).start()
-
-                @pl.when(jnp.logical_not(here))
-                def _():
+    for some in ((0, 1, 7, 2, 6), (3, 5, 4)):
+        for dz in some:
+            if dz:
+                arrived(attn.at[dz], a_r.at[dz])
+        rows = jnp.concatenate([attn[n] for n in some], axis=0)
+        for i in (2, 3, 1, 0):
+            j = (quarter + i) % 4
+            res = jnp.dot(rows, wbuf[j], preferred_element_type=F32).astype(BF)
+            for m, n in enumerate(some):
+                prod[i, n] = res[m * ROWS : (m + 1) * ROWS, :]
+            for n in some:
+                if i:
                     term_copy(i, n).start()
+                else:
+                    here = (z + n) % RINGZ == kvh
+
+                    @pl.when(here)
+                    def _():
+                        own_term(n).start()
+
+                    @pl.when(jnp.logical_not(here))
+                    def _():
+                        term_copy(i, n).start()
 
     for copy in out_swaps + [w_relay(partner)]:
         copy.wait_send()

time: 53.3 us -> 53.3 us (level)
  no operation moved by 1% of the time
where the time goes in v6:
time: 53.3 us; the launch traced here: 53.2 us
  Pallas kernels  51.5 us (97%)
  other arithmetic  1.61 us (3%)
    pallas_call x1, Pallas kernels, local(): pl.pallas_call(kernel, out_shape=jax.ShapeDtypeStruct((4 * RINGZ, ROWS, C...  51.5 us
    reduce_sum x1, other arithmetic, local(): return jnp.sum(terms, axis=0).astype(BF)  1.61 us

profile of v6, /device:TPU:1, one launch (start us, length us, event | category | flops | bytes accessed | tf_op | source)
XLA Modules:
  0.0 53.2 jit_solution(10460237925586181646)
XLA Ops:
  0.0 51.5 %shard_map.91 = bf16[32,16,256]{2,1,0:T(8,128)(2,1)} custom-call(bf16[16,1024]{1,0:T(8,128)(2,1)} %q_hbm.1, bf16[2048,128]{1,0:T(8,128)(2,1)} %k_hbm.1, bf16[2048,128]{1,0:T(8,128)(2,1)} %v_hbm.1, bf16[16,128]{1,0:T(8,128)(2,1)} %ck_hbm.1, bf16[16,128]{1,0:T(8,128)(2,1)} %cv_hbm.1, s32[16]{0:T(128)} %len_hbm.1, s32[16]{0:T(128)} %branch_hbm.1, s32[16]{0:T(128)} %depth_hbm.1, ...), custom_call_target="tpu_custom_call" | custom-call | flops 8999999488 | bytes 2097152 | tf_op jit(solution)/shard_map/pallas_call | solution.py:474
  51.5 1.6 %bitcast_reduce_fusion = bf16[64,256]{1,0:T(8,128)(2,1)} fusion(bf16[8,64,256]{2,1,0:T(8,128)(2,1)} %bitcast.3), kind=kLoop, calls=%fused_computation | loop fusion | flops 114688 | bytes 294912 | tf_op jit(solution)/shard_map/reduce_sum | solution.py:514
